TPU v7x, 512 devices: a whole 4x4x16 slice. The times are simulated.
512 devices in a mesh: group: 8 (over y, core), box: 64 (over z, x).
Axes of the slice: x: 4, y: 4, z: 16, core: 2. Of those that a mesh axis runs over, the one named last changes fastest.
Arguments:
- old_state: float32 [2, 9, 32, 1024, 128], P(None, None, 'group', 'box'), may hold values from -6 to 6
- owners: int32 [8, 2, 64], P('group'), may hold values from 0 to 63, as said below
- diffusivity: bfloat16 [9, 32, 1024, 128], P(None, 'group', 'box'), may hold values from 0.25 to 4
Outputs:
- smoothed: float32 [9, 32, 1024, 128], P(None, 'group', 'box')
Inputs may be any that keep to these rules, and one draw needn't show every extreme that they name: owners[g, 0, j] is the index along the cluster of the device that holds box j before the regrid and owners[g, 1, j] its slot (0 or 1). The old owner lies in the same aligned block of 4 boxes as j; no two boxes share an owner and a slot; in the first block of every cluster one device holds two boxes and some box's old owner differs from it in both of the two lowest bits of the index.
All inputs are finite; a program needn't handle non-finite values.
Results may differ from a plain program's by a relative error of at most 0.0003.
Values may be sent and summed in bfloat16 or wider, within the bound.
A program may use at most 64 MiB of HBM per device.

v0:
```python
import jax
import jax.numpy as jnp
from jax import lax
from jax.sharding import PartitionSpec as P

ITERS = 4


relax_weight = 0.5


def with_halo(x, sides, width):
    for axis, dim in sides:
        size, length = (lax.axis_size(axis), x.shape[dim])
        up = [(i, (i + 1) % size) for i in range(size - 1)]
        down = [(j, i) for i, j in up]
        last = lax.slice_in_dim(x, length - width, length, axis=dim)
        leading = lax.slice_in_dim(x, 0, width, axis=dim)
        before = lax.ppermute(last, axis, up)
        after = lax.ppermute(leading, axis, down)
        x = jnp.concatenate([before, x, after], axis=dim)
    return x


def interior(array):
    return array[..., 1:-1, 1:-1, :]


def face_terms(padded):
    center = interior(padded)
    return (
        0.5 * (center + padded[..., :-2, 1:-1, :]),
        0.5 * (center + padded[..., 2:, 1:-1, :]),
        0.5 * (center + padded[..., 1:-1, :-2, :]),
        0.5 * (center + padded[..., 1:-1, 2:, :]),
        0.5 * (center + jnp.roll(center, 1, axis=-1)),
        0.5 * (center + jnp.roll(center, -1, axis=-1)),
    )


def neighbour_sum(beside_all, face_set):
    center = interior(beside_all)
    total = face_set[0] * beside_all[..., :-2, 1:-1, :] + face_set[1] * beside_all[..., 2:, 1:-1, :]
    total = (
        total
        + face_set[2] * beside_all[..., 1:-1, :-2, :]
        + face_set[3] * beside_all[..., 1:-1, 2:, :]
    )
    total = (
        total
        + face_set[4] * jnp.roll(center, 1, axis=-1)
        + face_set[5] * jnp.roll(center, -1, axis=-1)
    )
    return total


def relax_step(beside_all, source, face_set, diagonal):
    return (source + relax_weight * neighbour_sum(beside_all, face_set)) / diagonal


def diagonal_of(face_set):
    return 1.0 + relax_weight * (
        face_set[0] + face_set[1] + face_set[2] + face_set[3] + face_set[4] + face_set[5]
    )


def local(old_state, owners, diffusivity):
    holder = owners[0, 0, :]
    slot_of = owners[0, 1, :]
    boxes_count = lax.axis_size("box")
    flattened = old_state.reshape(old_state.shape[0], boxes_count, -1)
    spread = lax.all_to_all(flattened, "box", split_axis=1, concat_axis=1, tiled=True)
    piece_pool = spread.reshape(old_state.shape[0] * boxes_count, flattened.shape[2])
    wanted = jnp.take(piece_pool, slot_of * boxes_count + holder, axis=0)
    gathered = lax.all_to_all(wanted, "box", split_axis=0, concat_axis=0, tiled=True)
    species = gathered.reshape(old_state.shape[1:])
    coef_pad = with_halo(diffusivity, (("group", 1), ("box", 2)), 1).astype(jnp.float32)
    face_set = face_terms(coef_pad)
    diagonal = diagonal_of(face_set)
    current = species
    for repeat in range(ITERS):
        beside_all = with_halo(current, (("group", 1), ("box", 2)), 1)
        current = relax_step(beside_all, species, face_set, diagonal)
    return current


def solution(mesh):
    placed = (
        P(None, None, "group", "box", None),
        P("group", None, None),
        P(None, "group", "box", None),
    )
    return jax.shard_map(
        local, mesh=mesh, in_specs=placed, out_specs=P(None, "group", "box", None), check_vma=False
    )
```

profile of v0, /device:TPU:103, one launch (start us, length us, event | category | flops | bytes accessed | tf_op | source)
XLA Modules:
  0.0 161.9 jit_solution(10132759492422809751)
XLA Ops:
  0.0 1.2 reshape.78
  1.2 1.3 copy.6
  2.5 16.8 %all-to-all-start = ((f32[2,64,1152]{2,0,1:T(2,128)}), f32[2,64,1152]{2,0,1:T(2,128)S(1)}, u32[]{:S(2)}, u32[]{:S(2)}) async-start(f32[2,64,1152]{2,0,1:T(2,128)} %copy.6), calls=%async_computation | async-start | bytes 1179648 | tf_op jit(solution)/shard_map/all_to_all | solution.py:72
  19.3 0.0 copy-start.1
  19.3 3.1 %collective-permute-start.1 = (bf16[9,1,16,128]{3,2,1,0:T(8,128)(2,1)S(1)}, bf16[9,1,16,128]{3,2,1,0:T(8,128)(2,1)S(1)}, u32[]{:S(2)}, u32[]{:S(2)}) collective-permute-start(bf16[9,1,16,128]{3,2,1,0:T(8,128)(2,1)S(1)} %get-tuple-element.52), channel_id=1, source_target_pairs={{64,0},{128,64},{192,128},{256,192},{320,256},{384,320},{448,384},... | collective-permute-start | bytes 110600 | tf_op jit(solution)/shard_map/ppermute | solution.py:20
  22.5 3.1 %collective-permute-start = (bf16[9,1,16,128]{3,2,1,0:T(8,128)(2,1)S(1)}, bf16[9,1,16,128]{3,2,1,0:T(8,128)(2,1)S(1)}, u32[]{:S(2)}, u32[]{:S(2)}) collective-permute-start(bf16[9,1,16,128]{3,2,1,0:T(8,128)(2,1)S(1)} %get-tuple-element.53), channel_id=1, source_target_pairs={{0,64},{64,128},{128,192},{192,256},{256,320},{320,384},{384,448},... | collective-permute-start | bytes 110600 | tf_op jit(solution)/shard_map/ppermute | solution.py:19
  25.6 26.4 %all-to-all-done = f32[2,64,1152]{2,0,1:T(2,128)S(1)} async-done(((f32[2,64,1152]{2,0,1:T(2,128)}), f32[2,64,1152]{2,0,1:T(2,128)S(1)}, u32[]{:S(2)}, u32[]{:S(2)}) %all-to-all-start) | async-done | bytes 589856 | tf_op jit(solution)/shard_map/all_to_all | solution.py:72
  52.1 0.7 gather_fusion
  52.8 0.1 bitcast_select_fusion
  52.9 1.0 copy.8
  53.9 7.9 %all-to-all-start.1 = ((f32[64,1,1152]{2,1,0:T(1,128)}), f32[64,1,1152]{2,1,0:T(1,128)S(1)}, u32[]{:S(2)}, u32[]{:S(2)}) async-start(f32[64,1,1152]{2,1,0:T(1,128)} %copy.8), calls=%async_computation.1 | async-start | bytes 589824 | tf_op jit(solution)/shard_map/all_to_all | solution.py:75
  61.8 0.0 collective-permute-done
  61.9 0.0 collective-permute-done.1
  61.9 4.3 %collective-permute-start.2 = (bf16[9,6,1,128]{3,2,1,0:T(2,128)(2,1)S(1)}, bf16[9,6,1,128]{3,2,1,0:T(2,128)(2,1)S(1)}, u32[]{:S(2)}, u32[]{:S(2)}) collective-permute-start(bf16[9,6,1,128]{3,2,1,0:T(2,128)(2,1)S(1)} %get-tuple-element.50), channel_id=1, source_target_pairs={{0,1},{1,2},{2,3},{3,4},{4,5},{5,6},{6,7},{7,8},{8,9},{9,10},{10,1... | collective-permute-start | bytes 41480 | tf_op jit(solution)/shard_map/ppermute | solution.py:19
  66.3 1.9 %collective-permute-start.3 = (bf16[9,6,1,128]{3,2,1,0:T(2,128)(2,1)S(1)}, bf16[9,6,1,128]{3,2,1,0:T(2,128)(2,1)S(1)}, u32[]{:S(2)}, u32[]{:S(2)}) collective-permute-start(bf16[9,6,1,128]{3,2,1,0:T(2,128)(2,1)S(1)} %get-tuple-element.51), channel_id=1, source_target_pairs={{1,0},{2,1},{3,2},{4,3},{5,4},{6,5},{7,6},{8,7},{9,8},{10,9},{11,1... | collective-permute-start | bytes 41480 | tf_op jit(solution)/shard_map/ppermute | solution.py:20
  68.2 6.5 %collective-permute-done.2 = bf16[9,6,1,128]{3,2,1,0:T(2,128)(2,1)S(1)} collective-permute-done((bf16[9,6,1,128]{3,2,1,0:T(2,128)(2,1)S(1)}, bf16[9,6,1,128]{3,2,1,0:T(2,128)(2,1)S(1)}, u32[]{:S(2)}, u32[]{:S(2)}) %collective-permute-start.2) | collective-permute-done | bytes 13856 | tf_op jit(solution)/shard_map/ppermute | solution.py:19
  74.6 0.8 collective-permute-done.3
  75.5 0.2 maximum_convert_fusion
  75.6 0.1 fusion.62
  75.8 0.1 fusion.61
  75.9 4.3 %all-to-all-done.1 = f32[64,1,1152]{2,1,0:T(1,128)S(1)} async-done(((f32[64,1,1152]{2,1,0:T(1,128)}), f32[64,1,1152]{2,1,0:T(1,128)S(1)}, u32[]{:S(2)}, u32[]{:S(2)}) %all-to-all-start.1) | async-done | bytes 294944 | tf_op jit(solution)/shard_map/all_to_all | solution.py:75
  80.2 6.2 %collective-permute-start.4 = (f32[9,1,16,128]{3,2,1,0:T(8,128)S(1)}, f32[9,1,16,128]{3,2,1,0:T(8,128)S(1)}, u32[]{:S(2)}, u32[]{:S(2)}) collective-permute-start(f32[9,1,16,128]{3,2,1,0:T(8,128)S(1)} %get-tuple-element.48), channel_id=1, source_target_pairs={{0,64},{64,128},{128,192},{192,256},{256,320},{320,384},{384,448},... | collective-permute-start | bytes 221192 | tf_op jit(solution)/shard_map/ppermute | solution.py:19
  86.4 1.9 %collective-permute-start.5 = (f32[9,1,16,128]{3,2,1,0:T(8,128)S(1)}, f32[9,1,16,128]{3,2,1,0:T(8,128)S(1)}, u32[]{:S(2)}, u32[]{:S(2)}) collective-permute-start(f32[9,1,16,128]{3,2,1,0:T(8,128)S(1)} %get-tuple-element.49), channel_id=1, source_target_pairs={{64,0},{128,64},{192,128},{256,192},{320,256},{384,320},{448,384},... | collective-permute-start | bytes 221192 | tf_op jit(solution)/shard_map/ppermute | solution.py:20
  88.3 0.1 fusion.72
  88.5 0.0 collective-permute-done.4
  88.5 3.6 %collective-permute-done.5 = f32[9,1,16,128]{3,2,1,0:T(8,128)S(1)} collective-permute-done((f32[9,1,16,128]{3,2,1,0:T(8,128)S(1)}, f32[9,1,16,128]{3,2,1,0:T(8,128)S(1)}, u32[]{:S(2)}, u32[]{:S(2)}) %collective-permute-start.5) | collective-permute-done | bytes 73760 | tf_op jit(solution)/shard_map/ppermute | solution.py:20
  92.1 2.9 %collective-permute-start.6 = (f32[9,6,1,128]{3,2,1,0:T(1,128)S(1)}, f32[9,6,1,128]{3,2,1,0:T(1,128)S(1)}, u32[]{:S(2)}, u32[]{:S(2)}) collective-permute-start(f32[9,6,1,128]{3,2,1,0:T(1,128)S(1)} %get-tuple-element.24), channel_id=1, source_target_pairs={{0,1},{1,2},{2,3},{3,4},{4,5},{5,6},{6,7},{7,8},{8,9},{9,10},{10,1... | collective-permute-start | bytes 82952 | tf_op jit(solution)/shard_map/ppermute | solution.py:19
  95.1 2.3 %collective-permute-start.7 = (f32[9,6,1,128]{3,2,1,0:T(1,128)S(1)}, f32[9,6,1,128]{3,2,1,0:T(1,128)S(1)}, u32[]{:S(2)}, u32[]{:S(2)}) collective-permute-start(f32[9,6,1,128]{3,2,1,0:T(1,128)S(1)} %get-tuple-element.25), channel_id=1, source_target_pairs={{1,0},{2,1},{3,2},{4,3},{5,4},{6,5},{7,6},{8,7},{9,8},{10,9},{11,1... | collective-permute-start | bytes 82952 | tf_op jit(solution)/shard_map/ppermute | solution.py:20
  97.4 0.1 fusion.73
  97.5 0.0 collective-permute-done.6
  97.6 5.4 %collective-permute-done.7 = f32[9,6,1,128]{3,2,1,0:T(1,128)S(1)} collective-permute-done((f32[9,6,1,128]{3,2,1,0:T(1,128)S(1)}, f32[9,6,1,128]{3,2,1,0:T(1,128)S(1)}, u32[]{:S(2)}, u32[]{:S(2)}) %collective-permute-start.7) | collective-permute-done | bytes 27680 | tf_op jit(solution)/shard_map/ppermute | solution.py:20
  103.0 0.7 fusion.42
  103.7 3.3 %collective-permute-start.8 = (f32[9,1,16,128]{3,2,1,0:T(8,128)S(1)}, f32[9,1,16,128]{3,2,1,0:T(8,128)S(1)}, u32[]{:S(2)}, u32[]{:S(2)}) collective-permute-start(f32[9,1,16,128]{3,2,1,0:T(8,128)S(1)} %get-tuple-element.42), channel_id=1, source_target_pairs={{0,64},{64,128},{128,192},{192,256},{256,320},{320,384},{384,448},... | collective-permute-start | bytes 221192 | tf_op jit(solution)/shard_map/ppermute | solution.py:19
  107.0 1.9 %collective-permute-start.9 = (f32[9,1,16,128]{3,2,1,0:T(8,128)S(1)}, f32[9,1,16,128]{3,2,1,0:T(8,128)S(1)}, u32[]{:S(2)}, u32[]{:S(2)}) collective-permute-start(f32[9,1,16,128]{3,2,1,0:T(8,128)S(1)} %get-tuple-element.43), channel_id=1, source_target_pairs={{64,0},{128,64},{192,128},{256,192},{320,256},{384,320},{448,384},... | collective-permute-start | bytes 221192 | tf_op jit(solution)/shard_map/ppermute | solution.py:20
  108.9 0.1 fusion.70
  109.1 0.0 collective-permute-done.8
  109.1 3.6 %collective-permute-done.9 = f32[9,1,16,128]{3,2,1,0:T(8,128)S(1)} collective-permute-done((f32[9,1,16,128]{3,2,1,0:T(8,128)S(1)}, f32[9,1,16,128]{3,2,1,0:T(8,128)S(1)}, u32[]{:S(2)}, u32[]{:S(2)}) %collective-permute-start.9) | collective-permute-done | bytes 73760 | tf_op jit(solution)/shard_map/ppermute | solution.py:20
  112.7 1.9 %collective-permute-start.10 = (f32[9,6,1,128]{3,2,1,0:T(1,128)S(1)}, f32[9,6,1,128]{3,2,1,0:T(1,128)S(1)}, u32[]{:S(2)}, u32[]{:S(2)}) collective-permute-start(f32[9,6,1,128]{3,2,1,0:T(1,128)S(1)} %get-tuple-element.22), channel_id=1, source_target_pairs={{0,1},{1,2},{2,3},{3,4},{4,5},{5,6},{6,7},{7,8},{8,9},{9,10},{10,1... | collective-permute-start | bytes 82952 | tf_op jit(solution)/shard_map/ppermute | solution.py:19
  114.7 3.4 %collective-permute-start.11 = (f32[9,6,1,128]{3,2,1,0:T(1,128)S(1)}, f32[9,6,1,128]{3,2,1,0:T(1,128)S(1)}, u32[]{:S(2)}, u32[]{:S(2)}) collective-permute-start(f32[9,6,1,128]{3,2,1,0:T(1,128)S(1)} %get-tuple-element.23), channel_id=1, source_target_pairs={{1,0},{2,1},{3,2},{4,3},{5,4},{6,5},{7,6},{8,7},{9,8},{10,9},{11,1... | collective-permute-start | bytes 82952 | tf_op jit(solution)/shard_map/ppermute | solution.py:20
  118.0 0.1 fusion.69
  118.2 0.0 collective-permute-done.10
  118.2 4.4 %collective-permute-done.11 = f32[9,6,1,128]{3,2,1,0:T(1,128)S(1)} collective-permute-done((f32[9,6,1,128]{3,2,1,0:T(1,128)S(1)}, f32[9,6,1,128]{3,2,1,0:T(1,128)S(1)}, u32[]{:S(2)}, u32[]{:S(2)}) %collective-permute-start.11) | collective-permute-done | bytes 27680 | tf_op jit(solution)/shard_map/ppermute | solution.py:20
  122.6 0.5 fusion.30
  123.1 3.0 %collective-permute-start.12 = (f32[9,1,16,128]{3,2,1,0:T(8,128)S(1)}, f32[9,1,16,128]{3,2,1,0:T(8,128)S(1)}, u32[]{:S(2)}, u32[]{:S(2)}) collective-permute-start(f32[9,1,16,128]{3,2,1,0:T(8,128)S(1)} %get-tuple-element.36), channel_id=1, source_target_pairs={{0,64},{64,128},{128,192},{192,256},{256,320},{320,384},{384,448},... | collective-permute-start | bytes 221192 | tf_op jit(solution)/shard_map/ppermute | solution.py:19
  126.1 1.9 %collective-permute-start.13 = (f32[9,1,16,128]{3,2,1,0:T(8,128)S(1)}, f32[9,1,16,128]{3,2,1,0:T(8,128)S(1)}, u32[]{:S(2)}, u32[]{:S(2)}) collective-permute-start(f32[9,1,16,128]{3,2,1,0:T(8,128)S(1)} %get-tuple-element.37), channel_id=1, source_target_pairs={{64,0},{128,64},{192,128},{256,192},{320,256},{384,320},{448,384},... | collective-permute-start | bytes 221192 | tf_op jit(solution)/shard_map/ppermute | solution.py:20
  128.0 0.1 fusion.67
  128.2 0.0 collective-permute-done.12
  128.2 3.6 %collective-permute-done.13 = f32[9,1,16,128]{3,2,1,0:T(8,128)S(1)} collective-permute-done((f32[9,1,16,128]{3,2,1,0:T(8,128)S(1)}, f32[9,1,16,128]{3,2,1,0:T(8,128)S(1)}, u32[]{:S(2)}, u32[]{:S(2)}) %collective-permute-start.13) | collective-permute-done | bytes 73760 | tf_op jit(solution)/shard_map/ppermute | solution.py:20
  131.8 1.9 %collective-permute-start.14 = (f32[9,6,1,128]{3,2,1,0:T(1,128)S(1)}, f32[9,6,1,128]{3,2,1,0:T(1,128)S(1)}, u32[]{:S(2)}, u32[]{:S(2)}) collective-permute-start(f32[9,6,1,128]{3,2,1,0:T(1,128)S(1)} %get-tuple-element.20), channel_id=1, source_target_pairs={{0,1},{1,2},{2,3},{3,4},{4,5},{5,6},{6,7},{7,8},{8,9},{9,10},{10,1... | collective-permute-start | bytes 82952 | tf_op jit(solution)/shard_map/ppermute | solution.py:19
  133.7 3.4 %collective-permute-start.15 = (f32[9,6,1,128]{3,2,1,0:T(1,128)S(1)}, f32[9,6,1,128]{3,2,1,0:T(1,128)S(1)}, u32[]{:S(2)}, u32[]{:S(2)}) collective-permute-start(f32[9,6,1,128]{3,2,1,0:T(1,128)S(1)} %get-tuple-element.21), channel_id=1, source_target_pairs={{1,0},{2,1},{3,2},{4,3},{5,4},{6,5},{7,6},{8,7},{9,8},{10,9},{11,1... | collective-permute-start | bytes 82952 | tf_op jit(solution)/shard_map/ppermute | solution.py:20
  137.1 0.1 fusion.66
  137.2 0.0 collective-permute-done.14
  137.3 4.4 %collective-permute-done.15 = f32[9,6,1,128]{3,2,1,0:T(1,128)S(1)} collective-permute-done((f32[9,6,1,128]{3,2,1,0:T(1,128)S(1)}, f32[9,6,1,128]{3,2,1,0:T(1,128)S(1)}, u32[]{:S(2)}, u32[]{:S(2)}) %collective-permute-start.15) | collective-permute-done | bytes 27680 | tf_op jit(solution)/shard_map/ppermute | solution.py:20
  141.7 0.5 fusion.18
  142.2 3.0 %collective-permute-start.16 = (f32[9,1,16,128]{3,2,1,0:T(8,128)S(1)}, f32[9,1,16,128]{3,2,1,0:T(8,128)S(1)}, u32[]{:S(2)}, u32[]{:S(2)}) collective-permute-start(f32[9,1,16,128]{3,2,1,0:T(8,128)S(1)} %get-tuple-element.30), channel_id=1, source_target_pairs={{0,64},{64,128},{128,192},{192,256},{256,320},{320,384},{384,448},... | collective-permute-start | bytes 221192 | tf_op jit(solution)/shard_map/ppermute | solution.py:19
  145.2 1.9 %collective-permute-start.17 = (f32[9,1,16,128]{3,2,1,0:T(8,128)S(1)}, f32[9,1,16,128]{3,2,1,0:T(8,128)S(1)}, u32[]{:S(2)}, u32[]{:S(2)}) collective-permute-start(f32[9,1,16,128]{3,2,1,0:T(8,128)S(1)} %get-tuple-element.31), channel_id=1, source_target_pairs={{64,0},{128,64},{192,128},{256,192},{320,256},{384,320},{448,384},... | collective-permute-start | bytes 221192 | tf_op jit(solution)/shard_map/ppermute | solution.py:20
  147.1 0.1 fusion.64
  147.3 0.0 collective-permute-done.16
  147.3 3.6 %collective-permute-done.17 = f32[9,1,16,128]{3,2,1,0:T(8,128)S(1)} collective-permute-done((f32[9,1,16,128]{3,2,1,0:T(8,128)S(1)}, f32[9,1,16,128]{3,2,1,0:T(8,128)S(1)}, u32[]{:S(2)}, u32[]{:S(2)}) %collective-permute-start.17) | collective-permute-done | bytes 73760 | tf_op jit(solution)/shard_map/ppermute | solution.py:20
  150.9 1.9 %collective-permute-start.18 = (f32[9,6,1,128]{3,2,1,0:T(1,128)S(1)}, f32[9,6,1,128]{3,2,1,0:T(1,128)S(1)}, u32[]{:S(2)}, u32[]{:S(2)}) collective-permute-start(f32[9,6,1,128]{3,2,1,0:T(1,128)S(1)} %get-tuple-element.18), channel_id=1, source_target_pairs={{0,1},{1,2},{2,3},{3,4},{4,5},{5,6},{6,7},{7,8},{8,9},{9,10},{10,1... | collective-permute-start | bytes 82952 | tf_op jit(solution)/shard_map/ppermute | solution.py:19
  152.8 3.4 %collective-permute-start.19 = (f32[9,6,1,128]{3,2,1,0:T(1,128)S(1)}, f32[9,6,1,128]{3,2,1,0:T(1,128)S(1)}, u32[]{:S(2)}, u32[]{:S(2)}) collective-permute-start(f32[9,6,1,128]{3,2,1,0:T(1,128)S(1)} %get-tuple-element.19), channel_id=1, source_target_pairs={{1,0},{2,1},{3,2},{4,3},{5,4},{6,5},{7,6},{8,7},{9,8},{10,9},{11,1... | collective-permute-start | bytes 82952 | tf_op jit(solution)/shard_map/ppermute | solution.py:20
  156.2 0.1 fusion.63
  156.4 4.4 %collective-permute-done.19 = f32[9,6,1,128]{3,2,1,0:T(1,128)S(1)} collective-permute-done((f32[9,6,1,128]{3,2,1,0:T(1,128)S(1)}, f32[9,6,1,128]{3,2,1,0:T(1,128)S(1)}, u32[]{:S(2)}, u32[]{:S(2)}) %collective-permute-start.19) | collective-permute-done | bytes 27680 | tf_op jit(solution)/shard_map/ppermute | solution.py:20
  160.8 1.2 fusion.6
  (21 shorter events, 0.4 us)
Async XLA Ops:
  2.5 16.8 %copy-start = (bf16[9,4,16,128]{3,2,1,0:T(8,128)(2,1)S(1)}, bf16[9,4,16,128]{3,2,1,0:T(8,128)(2,1)}, u32[]{:S(2)}) copy-start(bf16[9,4,16,128]{3,2,1,0:T(8,128)(2,1)} %param.5) | copy-start | bytes 442372
  2.5 49.6 %all-to-all-start = ((f32[2,64,1152]{2,0,1:T(2,128)}), f32[2,64,1152]{2,0,1:T(2,128)S(1)}, u32[]{:S(2)}, u32[]{:S(2)}) async-start(f32[2,64,1152]{2,0,1:T(2,128)} %copy.6), calls=%async_computation | async-start | bytes 1179648 | tf_op jit(solution)/shard_map/all_to_all | solution.py:72
  19.3 6.3 %copy-start.1 = (s32[1,2,64]{2,1,0:T(2,128)S(1)}, s32[1,2,64]{2,1,0:T(2,128)}, u32[]{:S(2)}) copy-start(s32[1,2,64]{2,1,0:T(2,128)} %param.4) | copy-start | bytes 1540
  19.3 42.6 %collective-permute-start.1 = (bf16[9,1,16,128]{3,2,1,0:T(8,128)(2,1)S(1)}, bf16[9,1,16,128]{3,2,1,0:T(8,128)(2,1)S(1)}, u32[]{:S(2)}, u32[]{:S(2)}) collective-permute-start(bf16[9,1,16,128]{3,2,1,0:T(8,128)(2,1)S(1)} %get-tuple-element.52), channel_id=1, source_target_pairs={{64,0},{128,64},{192,128},{256,192},{320,256},{384,320},{448,384},... | collective-permute-start | bytes 110600 | tf_op jit(solution)/shard_map/ppermute | solution.py:20
  22.5 39.4 %collective-permute-start = (bf16[9,1,16,128]{3,2,1,0:T(8,128)(2,1)S(1)}, bf16[9,1,16,128]{3,2,1,0:T(8,128)(2,1)S(1)}, u32[]{:S(2)}, u32[]{:S(2)}) collective-permute-start(bf16[9,1,16,128]{3,2,1,0:T(8,128)(2,1)S(1)} %get-tuple-element.53), channel_id=1, source_target_pairs={{0,64},{64,128},{128,192},{192,256},{256,320},{320,384},{384,448},... | collective-permute-start | bytes 110600 | tf_op jit(solution)/shard_map/ppermute | solution.py:19
  53.9 26.3 %all-to-all-start.1 = ((f32[64,1,1152]{2,1,0:T(1,128)}), f32[64,1,1152]{2,1,0:T(1,128)S(1)}, u32[]{:S(2)}, u32[]{:S(2)}) async-start(f32[64,1,1152]{2,1,0:T(1,128)} %copy.8), calls=%async_computation.1 | async-start | bytes 589824 | tf_op jit(solution)/shard_map/all_to_all | solution.py:75
  61.9 12.7 %collective-permute-start.2 = (bf16[9,6,1,128]{3,2,1,0:T(2,128)(2,1)S(1)}, bf16[9,6,1,128]{3,2,1,0:T(2,128)(2,1)S(1)}, u32[]{:S(2)}, u32[]{:S(2)}) collective-permute-start(bf16[9,6,1,128]{3,2,1,0:T(2,128)(2,1)S(1)} %get-tuple-element.50), channel_id=1, source_target_pairs={{0,1},{1,2},{2,3},{3,4},{4,5},{5,6},{6,7},{7,8},{8,9},{9,10},{10,1... | collective-permute-start | bytes 41480 | tf_op jit(solution)/shard_map/ppermute | solution.py:19
  66.3 9.2 %collective-permute-start.3 = (bf16[9,6,1,128]{3,2,1,0:T(2,128)(2,1)S(1)}, bf16[9,6,1,128]{3,2,1,0:T(2,128)(2,1)S(1)}, u32[]{:S(2)}, u32[]{:S(2)}) collective-permute-start(bf16[9,6,1,128]{3,2,1,0:T(2,128)(2,1)S(1)} %get-tuple-element.51), channel_id=1, source_target_pairs={{1,0},{2,1},{3,2},{4,3},{5,4},{6,5},{7,6},{8,7},{9,8},{10,9},{11,1... | collective-permute-start | bytes 41480 | tf_op jit(solution)/shard_map/ppermute | solution.py:20
  80.2 8.2 %collective-permute-start.4 = (f32[9,1,16,128]{3,2,1,0:T(8,128)S(1)}, f32[9,1,16,128]{3,2,1,0:T(8,128)S(1)}, u32[]{:S(2)}, u32[]{:S(2)}) collective-permute-start(f32[9,1,16,128]{3,2,1,0:T(8,128)S(1)} %get-tuple-element.48), channel_id=1, source_target_pairs={{0,64},{64,128},{128,192},{192,256},{256,320},{320,384},{384,448},... | collective-permute-start | bytes 221192 | tf_op jit(solution)/shard_map/ppermute | solution.py:19
  86.4 5.7 %collective-permute-start.5 = (f32[9,1,16,128]{3,2,1,0:T(8,128)S(1)}, f32[9,1,16,128]{3,2,1,0:T(8,128)S(1)}, u32[]{:S(2)}, u32[]{:S(2)}) collective-permute-start(f32[9,1,16,128]{3,2,1,0:T(8,128)S(1)} %get-tuple-element.49), channel_id=1, source_target_pairs={{64,0},{128,64},{192,128},{256,192},{320,256},{384,320},{448,384},... | collective-permute-start | bytes 221192 | tf_op jit(solution)/shard_map/ppermute | solution.py:20
  92.1 5.4 %collective-permute-start.6 = (f32[9,6,1,128]{3,2,1,0:T(1,128)S(1)}, f32[9,6,1,128]{3,2,1,0:T(1,128)S(1)}, u32[]{:S(2)}, u32[]{:S(2)}) collective-permute-start(f32[9,6,1,128]{3,2,1,0:T(1,128)S(1)} %get-tuple-element.24), channel_id=1, source_target_pairs={{0,1},{1,2},{2,3},{3,4},{4,5},{5,6},{6,7},{7,8},{8,9},{9,10},{10,1... | collective-permute-start | bytes 82952 | tf_op jit(solution)/shard_map/ppermute | solution.py:19
  95.1 7.9 %collective-permute-start.7 = (f32[9,6,1,128]{3,2,1,0:T(1,128)S(1)}, f32[9,6,1,128]{3,2,1,0:T(1,128)S(1)}, u32[]{:S(2)}, u32[]{:S(2)}) collective-permute-start(f32[9,6,1,128]{3,2,1,0:T(1,128)S(1)} %get-tuple-element.25), channel_id=1, source_target_pairs={{1,0},{2,1},{3,2},{4,3},{5,4},{6,5},{7,6},{8,7},{9,8},{10,9},{11,1... | collective-permute-start | bytes 82952 | tf_op jit(solution)/shard_map/ppermute | solution.py:20
  103.7 5.4 %collective-permute-start.8 = (f32[9,1,16,128]{3,2,1,0:T(8,128)S(1)}, f32[9,1,16,128]{3,2,1,0:T(8,128)S(1)}, u32[]{:S(2)}, u32[]{:S(2)}) collective-permute-start(f32[9,1,16,128]{3,2,1,0:T(8,128)S(1)} %get-tuple-element.42), channel_id=1, source_target_pairs={{0,64},{64,128},{128,192},{192,256},{256,320},{320,384},{384,448},... | collective-permute-start | bytes 221192 | tf_op jit(solution)/shard_map/ppermute | solution.py:19
  107.0 5.7 %collective-permute-start.9 = (f32[9,1,16,128]{3,2,1,0:T(8,128)S(1)}, f32[9,1,16,128]{3,2,1,0:T(8,128)S(1)}, u32[]{:S(2)}, u32[]{:S(2)}) collective-permute-start(f32[9,1,16,128]{3,2,1,0:T(8,128)S(1)} %get-tuple-element.43), channel_id=1, source_target_pairs={{64,0},{128,64},{192,128},{256,192},{320,256},{384,320},{448,384},... | collective-permute-start | bytes 221192 | tf_op jit(solution)/shard_map/ppermute | solution.py:20
  112.7 5.4 %collective-permute-start.10 = (f32[9,6,1,128]{3,2,1,0:T(1,128)S(1)}, f32[9,6,1,128]{3,2,1,0:T(1,128)S(1)}, u32[]{:S(2)}, u32[]{:S(2)}) collective-permute-start(f32[9,6,1,128]{3,2,1,0:T(1,128)S(1)} %get-tuple-element.22), channel_id=1, source_target_pairs={{0,1},{1,2},{2,3},{3,4},{4,5},{5,6},{6,7},{7,8},{8,9},{9,10},{10,1... | collective-permute-start | bytes 82952 | tf_op jit(solution)/shard_map/ppermute | solution.py:19
  114.7 7.9 %collective-permute-start.11 = (f32[9,6,1,128]{3,2,1,0:T(1,128)S(1)}, f32[9,6,1,128]{3,2,1,0:T(1,128)S(1)}, u32[]{:S(2)}, u32[]{:S(2)}) collective-permute-start(f32[9,6,1,128]{3,2,1,0:T(1,128)S(1)} %get-tuple-element.23), channel_id=1, source_target_pairs={{1,0},{2,1},{3,2},{4,3},{5,4},{6,5},{7,6},{8,7},{9,8},{10,9},{11,1... | collective-permute-start | bytes 82952 | tf_op jit(solution)/shard_map/ppermute | solution.py:20
  123.1 5.1 %collective-permute-start.12 = (f32[9,1,16,128]{3,2,1,0:T(8,128)S(1)}, f32[9,1,16,128]{3,2,1,0:T(8,128)S(1)}, u32[]{:S(2)}, u32[]{:S(2)}) collective-permute-start(f32[9,1,16,128]{3,2,1,0:T(8,128)S(1)} %get-tuple-element.36), channel_id=1, source_target_pairs={{0,64},{64,128},{128,192},{192,256},{256,320},{320,384},{384,448},... | collective-permute-start | bytes 221192 | tf_op jit(solution)/shard_map/ppermute | solution.py:19
  126.1 5.7 %collective-permute-start.13 = (f32[9,1,16,128]{3,2,1,0:T(8,128)S(1)}, f32[9,1,16,128]{3,2,1,0:T(8,128)S(1)}, u32[]{:S(2)}, u32[]{:S(2)}) collective-permute-start(f32[9,1,16,128]{3,2,1,0:T(8,128)S(1)} %get-tuple-element.37), channel_id=1, source_target_pairs={{64,0},{128,64},{192,128},{256,192},{320,256},{384,320},{448,384},... | collective-permute-start | bytes 221192 | tf_op jit(solution)/shard_map/ppermute | solution.py:20
  131.8 5.4 %collective-permute-start.14 = (f32[9,6,1,128]{3,2,1,0:T(1,128)S(1)}, f32[9,6,1,128]{3,2,1,0:T(1,128)S(1)}, u32[]{:S(2)}, u32[]{:S(2)}) collective-permute-start(f32[9,6,1,128]{3,2,1,0:T(1,128)S(1)} %get-tuple-element.20), channel_id=1, source_target_pairs={{0,1},{1,2},{2,3},{3,4},{4,5},{5,6},{6,7},{7,8},{8,9},{9,10},{10,1... | collective-permute-start | bytes 82952 | tf_op jit(solution)/shard_map/ppermute | solution.py:19
  133.7 7.9 %collective-permute-start.15 = (f32[9,6,1,128]{3,2,1,0:T(1,128)S(1)}, f32[9,6,1,128]{3,2,1,0:T(1,128)S(1)}, u32[]{:S(2)}, u32[]{:S(2)}) collective-permute-start(f32[9,6,1,128]{3,2,1,0:T(1,128)S(1)} %get-tuple-element.21), channel_id=1, source_target_pairs={{1,0},{2,1},{3,2},{4,3},{5,4},{6,5},{7,6},{8,7},{9,8},{10,9},{11,1... | collective-permute-start | bytes 82952 | tf_op jit(solution)/shard_map/ppermute | solution.py:20
  142.2 5.1 %collective-permute-start.16 = (f32[9,1,16,128]{3,2,1,0:T(8,128)S(1)}, f32[9,1,16,128]{3,2,1,0:T(8,128)S(1)}, u32[]{:S(2)}, u32[]{:S(2)}) collective-permute-start(f32[9,1,16,128]{3,2,1,0:T(8,128)S(1)} %get-tuple-element.30), channel_id=1, source_target_pairs={{0,64},{64,128},{128,192},{192,256},{256,320},{320,384},{384,448},... | collective-permute-start | bytes 221192 | tf_op jit(solution)/shard_map/ppermute | solution.py:19
  145.2 5.7 %collective-permute-start.17 = (f32[9,1,16,128]{3,2,1,0:T(8,128)S(1)}, f32[9,1,16,128]{3,2,1,0:T(8,128)S(1)}, u32[]{:S(2)}, u32[]{:S(2)}) collective-permute-start(f32[9,1,16,128]{3,2,1,0:T(8,128)S(1)} %get-tuple-element.31), channel_id=1, source_target_pairs={{64,0},{128,64},{192,128},{256,192},{320,256},{384,320},{448,384},... | collective-permute-start | bytes 221192 | tf_op jit(solution)/shard_map/ppermute | solution.py:20
  150.9 5.4 %collective-permute-start.18 = (f32[9,6,1,128]{3,2,1,0:T(1,128)S(1)}, f32[9,6,1,128]{3,2,1,0:T(1,128)S(1)}, u32[]{:S(2)}, u32[]{:S(2)}) collective-permute-start(f32[9,6,1,128]{3,2,1,0:T(1,128)S(1)} %get-tuple-element.18), channel_id=1, source_target_pairs={{0,1},{1,2},{2,3},{3,4},{4,5},{5,6},{6,7},{7,8},{8,9},{9,10},{10,1... | collective-permute-start | bytes 82952 | tf_op jit(solution)/shard_map/ppermute | solution.py:19
  152.8 7.9 %collective-permute-start.19 = (f32[9,6,1,128]{3,2,1,0:T(1,128)S(1)}, f32[9,6,1,128]{3,2,1,0:T(1,128)S(1)}, u32[]{:S(2)}, u32[]{:S(2)}) collective-permute-start(f32[9,6,1,128]{3,2,1,0:T(1,128)S(1)} %get-tuple-element.19), channel_id=1, source_target_pairs={{1,0},{2,1},{3,2},{4,3},{5,4},{6,5},{7,6},{8,7},{9,8},{10,9},{11,1... | collective-permute-start | bytes 82952 | tf_op jit(solution)/shard_map/ppermute | solution.py:20
where the time goes:
time: 163 us; the launch traced here: 162 us
  starting transfers between devices  81.4 us (50%)
  waiting for transfers between devices  70.9 us (43%)
  local copies, waits for them, and re-layouts  5.8 us (4%)
  other arithmetic  3.3 us (2%)
    ppermute x10, waiting for transfers between devices, with_halo(): after = lax.ppermute(leading, axis, down)  33.8 us
    ppermute x10, starting transfers between devices, with_halo(): before = lax.ppermute(last, axis, up)  31.6 us
    all_to_all x1, waiting for transfers between devices, local(): lax.all_to_all(flattened, 'box', split_axis=1, concat_axis=1, tiled=True)  26.4 us
    ppermute x10, starting transfers between devices, with_halo(): after = lax.ppermute(leading, axis, down)  25.2 us
    all_to_all x1, starting transfers between devices, local(): lax.all_to_all(flattened, 'box', split_axis=1, concat_axis=1, tiled=True)  16.8 us
    all_to_all x1, starting transfers between devices, local(): lax.all_to_all(wanted, 'box', split_axis=0, concat_axis=0, tiled=True)  7.89 us
    ppermute x10, waiting for transfers between devices, with_halo(): before = lax.ppermute(last, axis, up)  6.49 us
    all_to_all x1, waiting for transfers between devices, local(): lax.all_to_all(wanted, 'box', split_axis=0, concat_axis=0, tiled=True)  4.26 us
  transfers between devices with their start and end apart: 22, of which 12 were waited for; matrix products, arithmetic and copies ran while one was open for 2% of the time, Pallas kernels for 0%

commit v1 on v0

v1 whole, which is shorter than its diff:
```python
import functools

import jax
import jax.numpy as jnp
from jax import lax
from jax.experimental import pallas as pl
from jax.experimental.pallas import tpu as pltpu
from jax.sharding import PartitionSpec as P

MESH = pl.DeviceIdType.MESH
BLOCK = 4
ITERS = 4
LEVELS = 32767.0
ZROWS = 24


def low_rows():
    return lax.broadcasted_iota(jnp.int32, (8, 128), 0) < 4


def pack_edges(rows):
    low = low_rows()
    first, last = [], []
    for a in (0, 2):
        p, q = rows[a], rows[a + 1]
        first.append(jnp.where(low, p[0:8], pltpu.roll(q[0:8], 4, 0)))
        last.append(jnp.where(low, pltpu.roll(p[8:16], 4, 0), q[8:16]))
    return jnp.concatenate(first, 0), jnp.concatenate(last, 0)


def unpack_edges(after, before):
    low = low_rows()
    out = []
    for a in range(4):
        n = after[8 * (a // 2):8 * (a // 2) + 8]
        p = before[8 * (a // 2):8 * (a // 2) + 8]
        if a % 2 == 0:
            out.append(jnp.where(low, n, pltpu.roll(p, 4, 0)))
        else:
            out.append(jnp.where(low, pltpu.roll(n, 4, 0), p))
    return out


def kernel(chunks, own_ref, old_ref, dif_ref, out_ref, old, enc, cand, recv, box, beside, edge, got_edge, corner,
           scl, scl_cand, scl_recv, scl_own, scl_got, dif, dif_edge, dif_beside, dif_got, dif_corner,
           coef, slab, cur, wts, res, sem_in, sem_out, sem_dif_in,
           s_send, s_recv, r_send, r_recv, h_send, h_recv, d_send, d_recv, n_send, n_recv):
    species = dif_ref.shape[0]
    g, b = lax.axis_index("group"), lax.axis_index("box")
    groups, boxes = lax.axis_size("group"), lax.axis_size("box")
    x = lax.rem(b, BLOCK)
    base = b - x
    ring = [None] + [(g, base + lax.rem(x + d, BLOCK)) for d in range(1, BLOCK)]
    gs = (lax.rem(g + groups - 1, groups), lax.rem(g + 1, groups))
    bs = (lax.rem(b + 1, boxes), lax.rem(b + boxes - 1, boxes))
    sides = [(gs[0], b), (gs[1], b)]
    ends = [(g, bs[0]), (g, bs[1])]
    diagonal = [[(gs[i], bs[j]) for j in range(2)] for i in range(2)]
    partners = ring[1:] + sides + ends + diagonal[0] + diagonal[1]

    loads = []
    for k, (s0, n) in enumerate(chunks):
        cp = pltpu.make_async_copy(old_ref.at[:, pl.ds(s0, n)], old[k], sem_in.at[k])
        cp.start()
        loads.append(cp)
    dif_load = pltpu.make_async_copy(dif_ref, dif, sem_dif_in)
    dif_load.start()

    barrier = pltpu.get_barrier_semaphore()
    for dev in partners:
        pl.semaphore_signal(barrier, inc=1, device_id=dev, device_id_type=MESH)

    def remote(src, dst, send, recv_sem, dev):
        return pltpu.make_async_remote_copy(src_ref=src, dst_ref=dst, send_sem=send, recv_sem=recv_sem,
                                            device_id=dev, device_id_type=MESH)

    slot = [own_ref[0, 1, base + lax.rem(x + d, BLOCK)] for d in range(BLOCK)]
    holder = own_ref[0, 0, b]
    came = lax.rem(lax.rem(holder, BLOCK) + BLOCK - x, BLOCK)

    dif_load.wait()

    def dif_pack(s, _):
        first, last = pack_edges([dif[s, a].astype(jnp.float32) for a in range(4)])
        dif_edge[0, s] = first.astype(jnp.bfloat16)
        dif_edge[1, s] = last.astype(jnp.bfloat16)
        return 0

    lax.fori_loop(0, species, dif_pack, 0)

    for cp in loads:
        cp.wait()
    for k, (s0, n) in enumerate(chunks):
        for t in range(2):
            for s in range(n):
                m = jnp.max(jnp.abs(old[k][t, s]), axis=0)
                m = jnp.max(m, axis=0, keepdims=True)
                scl[t, pl.ds(s0 + s, 1)] = jnp.maximum(m, 1e-30) * (1.0 / LEVELS)
    for d in range(1, BLOCK):
        scl_cand[d - 1] = scl[slot[d]]
    scl_recv[0] = scl[slot[0]]

    pl.semaphore_wait(barrier, len(partners))

    sends = []
    waits = {}

    def send(name, src, dst, send_sem, recv_sem, dev):
        cp = remote(src, dst, send_sem, recv_sem, dev)
        cp.start()
        sends.append(cp)
        waits.setdefault(name, []).append(cp)

    def arrive(name):
        for cp in waits.pop(name):
            cp.wait_recv()

    for e in range(2):
        send("dif_edge", dif_edge.at[e], dif_got.at[e], d_send.at[e], d_recv.at[e], ends[1 - e])
    for d in range(1, BLOCK):
        send("scl", scl_cand.at[d - 1], scl_recv.at[BLOCK - d], s_send.at[d - 1], s_recv.at[d - 1], ring[d])

    for k, (s0, n) in enumerate(chunks):

        def encode(s, _):
            for t in range(2):
                inv = 1.0 / scl[t, pl.ds(s0 + s, 1)]
                for a in range(4):
                    q = jnp.round(old[k][t, s, a] * inv).astype(jnp.int32)
                    enc[k][t, s, pl.ds(16 * a, 16)] = q.astype(jnp.int16)
            return 0

        lax.fori_loop(0, n, encode, 0)
        for d in range(BLOCK):
            if d:
                cand[k][d - 1] = enc[k][slot[d]]
                send(("regrid", k), cand[k].at[d - 1], recv[k].at[BLOCK - d], r_send.at[k, d - 1], r_recv.at[k, d - 1],
                     ring[d])
            else:
                recv[k][0] = enc[k][slot[0]]
    for i in range(2):
        send("dif_side", dif, dif_beside.at[i], d_send.at[2 + i], d_recv.at[2 + i], sides[1 - i])

    arrive("scl")
    scl_own[...] = scl_recv[came]
    for i in range(2):
        send("scl_all", scl_own, scl_got.at[i, 0], n_send.at[i], n_recv.at[i], sides[1 - i])
        send("scl_all", scl_own, scl_got.at[2, 1 + i], n_send.at[2 + i], n_recv.at[2 + i], ends[1 - i])
        for j in range(2):
            m = 4 + 2 * i + j
            send("scl_all", scl_own, scl_got.at[i, 1 + j], n_send.at[m], n_recv.at[m], diagonal[1 - i][1 - j])

    arrive("dif_edge")
    for i in range(2):
        send("dif_corner", dif_got, dif_corner.at[i], d_send.at[4 + i], d_recv.at[4 + i], sides[1 - i])

    for k, (s0, n) in enumerate(chunks):
        arrive(("regrid", k))

        def choose(s, _):
            q = recv[k][came, s]
            box[k][s] = q
            first, last = pack_edges([q[16 * a:16 * a + 16].astype(jnp.int32) for a in range(4)])
            edge[k][0, s] = first.astype(jnp.int16)
            edge[k][1, s] = last.astype(jnp.int16)
            return 0

        lax.fori_loop(0, n, choose, 0)
        for i in range(2):
            send(("halo", k), box[k], beside[k].at[i], h_send.at[k, i], h_recv.at[k, i], sides[1 - i])
        for e in range(2):
            send(("halo", k), edge[k].at[e], got_edge[k].at[e], h_send.at[k, 2 + e], h_recv.at[k, 2 + e], ends[1 - e])
        for i in range(2):
            for e in range(2):
                m = 4 + 2 * i + e
                send(("halo", k), edge[k].at[e], corner[k].at[i, e], h_send.at[k, m], h_recv.at[k, m],
                     diagonal[1 - i][1 - e])

    in_side = [(g > 0).astype(jnp.float32), (g < groups - 1).astype(jnp.float32)]
    in_end = [(b < boxes - 1).astype(jnp.float32), (b > 0).astype(jnp.float32)]
    row = lax.broadcasted_iota(jnp.int32, (ZROWS, 128), 0)
    in_rows = jnp.where(row < 16, 1.0, jnp.where(row < 20, in_end[0], in_end[1]))

    arrive("dif_side")
    arrive("dif_corner")

    def weigh(s, _):
        for part in range(3):
            for a in range(4):
                rows = dif[s, a] if part == 1 else dif_beside[0 if part == 0 else 1, s, a]
                rows = rows.astype(jnp.float32)
                if part != 1:
                    rows = rows * in_side[0 if part == 0 else 1]
                coef[4 * part + a, 0:16] = rows
            if part == 1:
                after, before = dif_got[0, s], dif_got[1, s]
                m = 1.0
            else:
                i = 0 if part == 0 else 1
                after, before = dif_corner[i, 0, s], dif_corner[i, 1, s]
                m = in_side[i]
            halo = unpack_edges(after.astype(jnp.float32) * (in_end[0] * m), before.astype(jnp.float32) * (in_end[1] * m))
            for a in range(4):
                coef[4 * part + a, 16:24] = halo[a]
        for a in range(1, 11):
            c = coef[a]
            faces = [c + coef[a - 1], c + coef[a + 1],
                     c + pltpu.roll(c, 1, 0), c + pltpu.roll(c, ZROWS - 1, 0),
                     c + pltpu.roll(c, 1, 1), c + pltpu.roll(c, 127, 1)]
            total = (faces[0] + faces[1]) + (faces[2] + faces[3]) + (faces[4] + faces[5])
            scale = in_rows / (1.0 + 0.25 * total)
            if a < 4:
                scale = scale * in_side[0]
            elif a > 7:
                scale = scale * in_side[1]
            wts[s, a - 1, 6] = scale
            scale = 0.25 * scale
            for f in range(6):
                wts[s, a - 1, f] = faces[f] * scale
        return 0

    lax.fori_loop(0, species, weigh, 0)
    arrive("scl_all")

    outs = []
    for k, (s0, n) in enumerate(chunks):
        arrive(("halo", k))

        def smooth(s, _):
            at = s0 + s
            for part in range(3):
                if part == 1:
                    q, after, before = box[k][s], got_edge[k][0, s], got_edge[k][1, s]
                    own_s, after_s, before_s = scl_own[pl.ds(at, 1)], scl_got[2, 1, pl.ds(at, 1)], scl_got[2, 2, pl.ds(at, 1)]
                    m = 1.0
                else:
                    i = 0 if part == 0 else 1
                    q, after, before = beside[k][i, s], corner[k][i, 0, s], corner[k][i, 1, s]
                    own_s, after_s, before_s = (scl_got[i, j, pl.ds(at, 1)] for j in range(3))
                    m = in_side[i]
                    own_s = own_s * m
                q = q.astype(jnp.int32).astype(jnp.float32) * own_s
                after = after.astype(jnp.int32).astype(jnp.float32) * (after_s * (in_end[0] * m))
                before = before.astype(jnp.int32).astype(jnp.float32) * (before_s * (in_end[1] * m))
                halo = unpack_edges(after, before)
                for a in range(4):
                    slab[4 * part + a, 0:16] = q[16 * a:16 * a + 16]
                    slab[4 * part + a, 16:24] = halo[a]
            for it in range(ITERS):
                src = slab if it == 0 else cur.at[(it - 1) % 2]
                for a in range(1 + it, 11 - it):
                    v = src[a]
                    own = slab[a] if it else v
                    w = [wts[at, a - 1, f] for f in range(7)]
                    acc = w[6] * own + w[0] * src[a - 1] + w[1] * src[a + 1]
                    acc = acc + w[2] * pltpu.roll(v, 1, 0) + w[3] * pltpu.roll(v, ZROWS - 1, 0)
                    acc = acc + w[4] * pltpu.roll(v, 1, 1) + w[5] * pltpu.roll(v, 127, 1)
                    if it == ITERS - 1:
                        res[at, a - 4] = acc[0:16]
                    else:
                        cur[it % 2, a] = acc
            return 0

        lax.fori_loop(0, n, smooth, 0)
        cp = pltpu.make_async_copy(res.at[pl.ds(s0, n)], out_ref.at[pl.ds(s0, n)], sem_out.at[k])
        cp.start()
        outs.append(cp)
    for cp in sends:
        cp.wait_send()
    for cp in outs:
        cp.wait()


def cut(species):
    if species >= 9:
        sizes = [3, 3, species - 6]
    else:
        sizes = [1] * species
    chunks, s0 = [], 0
    for n in sizes:
        chunks.append((s0, n))
        s0 += n
    return chunks


def local(old_state, owners, diffusivity):
    species = diffusivity.shape[0]
    chunks = cut(species)
    i16, bf16, f32 = jnp.int16, jnp.bfloat16, jnp.float32
    dma = pltpu.SemaphoreType.DMA
    nk = len(chunks)
    scratch = [
        [pltpu.VMEM((2, n, 4, 16, 128), f32) for _, n in chunks],
        [pltpu.VMEM((2, n, 64, 128), i16) for _, n in chunks],
        [pltpu.VMEM((3, n, 64, 128), i16) for _, n in chunks],
        [pltpu.VMEM((4, n, 64, 128), i16) for _, n in chunks],
        [pltpu.VMEM((n, 64, 128), i16) for _, n in chunks],
        [pltpu.VMEM((2, n, 64, 128), i16) for _, n in chunks],
        [pltpu.VMEM((2, n, 16, 128), i16) for _, n in chunks],
        [pltpu.VMEM((2, n, 16, 128), i16) for _, n in chunks],
        [pltpu.VMEM((2, 2, n, 16, 128), i16) for _, n in chunks],
        pltpu.VMEM((2, species, 128), f32),
        pltpu.VMEM((3, species, 128), f32),
        pltpu.VMEM((4, species, 128), f32),
        pltpu.VMEM((species, 128), f32),
        pltpu.VMEM((3, 3, species, 128), f32),
        pltpu.VMEM((species, 4, 16, 128), bf16),
        pltpu.VMEM((2, species, 16, 128), bf16),
        pltpu.VMEM((2, species, 4, 16, 128), bf16),
        pltpu.VMEM((2, species, 16, 128), bf16),
        pltpu.VMEM((2, 2, species, 16, 128), bf16),
        pltpu.VMEM((12, ZROWS, 128), f32),
        pltpu.VMEM((12, ZROWS, 128), f32),
        pltpu.VMEM((2, 12, ZROWS, 128), f32),
        pltpu.VMEM((species, 10, 7, ZROWS, 128), f32),
        pltpu.VMEM((species, 4, 16, 128), f32),
        dma((nk,)), dma((nk,)), dma(()),
        dma((3,)), dma((3,)), dma((nk, 3)), dma((nk, 3)), dma((nk, 8)), dma((nk, 8)),
        dma((6,)), dma((6,)), dma((8,)), dma((8,)),
    ]
    return pl.pallas_call(
        functools.partial(kernel, chunks),
        out_shape=jax.ShapeDtypeStruct(diffusivity.shape, f32),
        in_specs=[pl.BlockSpec(memory_space=pltpu.SMEM), pl.BlockSpec(memory_space=pl.ANY),
                  pl.BlockSpec(memory_space=pl.ANY)],
        out_specs=pl.BlockSpec(memory_space=pl.ANY),
        scratch_shapes=scratch,
        name="regrid_smooth",
        compiler_params=pltpu.CompilerParams(collective_id=0, has_side_effects=True, vmem_limit_bytes=40 * 2**20),
    )(owners, old_state, diffusivity)


def solution(mesh):
    placed = (
        P(None, None, "group", "box", None),
        P("group", None, None),
        P(None, "group", "box", None),
    )
    return jax.shard_map(
        local, mesh=mesh, in_specs=placed, out_specs=P(None, "group", "box", None), check_vma=False
    )
```

time: 163 us -> 38.9 us (0.24)
  the two profiles are of different devices: /device:TPU:103 before, /device:TPU:1 now
where the time goes in v1:
time: 38.9 us; the launch traced here: 38.7 us
  Pallas kernels  35.4 us (91%)
  local copies, waits for them, and re-layouts  3.37 us (9%)
    pallas_call x1, Pallas kernels, local(): pl.pallas_call(functools.partial(kernel, chunks), out_shape=jax.ShapeDtyp...  35.4 us
    unnamed x7, local copies, waits for them, and re-layouts  3.37 us

profile of v1, /device:TPU:1, one launch (start us, length us, event | category | flops | bytes accessed | tf_op | source)
XLA Modules:
  0.0 38.7 jit_solution(12805184923994963521)
XLA Ops:
  0.0 0.0 copy-start
  0.0 1.1 %copy-done = f32[2,9,4,16,128]{4,3,2,1,0:T(8,128)S(1)} copy-done((f32[2,9,4,16,128]{4,3,2,1,0:T(8,128)S(1)}, f32[2,9,4,16,128]{4,3,2,1,0:T(8,128)}, u32[]{:S(2)}) %copy-start) | copy-done | bytes 589848
  1.1 0.0 copy-start.1
  1.1 0.9 %copy-done.1 = bf16[9,4,16,128]{3,2,1,0:T(8,128)(2,1)S(1)} copy-done((bf16[9,4,16,128]{3,2,1,0:T(8,128)(2,1)S(1)}, bf16[9,4,16,128]{3,2,1,0:T(8,128)(2,1)}, u32[]{:S(2)}) %copy-start.1) | copy-done | bytes 147480
  2.0 0.0 copy-start.2
  2.0 0.7 %copy-done.2 = s32[1,2,64]{2,1,0:T(2,128)S(1)} copy-done((s32[1,2,64]{2,1,0:T(2,128)S(1)}, s32[1,2,64]{2,1,0:T(2,128)}, u32[]{:S(2)}) %copy-start.2) | copy-done | bytes 536
  2.7 35.4 %regrid_smooth.1 = f32[9,4,16,128]{3,2,1,0:T(8,128)S(1)} custom-call(s32[1,2,64]{2,1,0:T(2,128)S(1)} %copy-done.2, f32[2,9,4,16,128]{4,3,2,1,0:T(8,128)S(1)} %copy-done, bf16[9,4,16,128]{3,2,1,0:T(8,128)(2,1)S(1)} %copy-done.1), custom_call_target="tpu_custom_call" | custom-call | tf_op jit(solution)/shard_map/regrid_smooth/pallas_call | solution.py:321
  38.0 0.7 %copy.5 = f32[9,4,16,128]{3,2,1,0:T(8,128)} copy(f32[9,4,16,128]{3,2,1,0:T(8,128)S(1)} %regrid_smooth.1) | data formatting | bytes 589824
Async XLA Ops:
  0.0 1.1 %copy-start = (f32[2,9,4,16,128]{4,3,2,1,0:T(8,128)S(1)}, f32[2,9,4,16,128]{4,3,2,1,0:T(8,128)}, u32[]{:S(2)}) copy-start(f32[2,9,4,16,128]{4,3,2,1,0:T(8,128)} %old_ref.1) | copy-start | bytes 1769476
  1.1 0.9 %copy-start.1 = (bf16[9,4,16,128]{3,2,1,0:T(8,128)(2,1)S(1)}, bf16[9,4,16,128]{3,2,1,0:T(8,128)(2,1)}, u32[]{:S(2)}) copy-start(bf16[9,4,16,128]{3,2,1,0:T(8,128)(2,1)} %dif_ref.1) | copy-start | bytes 442372
  2.0 0.7 %copy-start.2 = (s32[1,2,64]{2,1,0:T(2,128)S(1)}, s32[1,2,64]{2,1,0:T(2,128)}, u32[]{:S(2)}) copy-start(s32[1,2,64]{2,1,0:T(2,128)} %own_ref.1) | copy-start | bytes 1540

commit v2 on v1

--- a/solution.py
+++ b/solution.py
@@ -12,6 +12,13 @@
 ITERS = 4
 LEVELS = 32767.0
 ZROWS = 24
+
+
+def when(condition, act):
+    if condition is None:
+        act()
+    else:
+        pl.when(condition)(act)
 
 
 def low_rows():
@@ -41,9 +48,9 @@
     return out
 
 
-def kernel(chunks, own_ref, old_ref, dif_ref, out_ref, old, enc, cand, recv, box, beside, edge, got_edge, corner,
+def kernel(chunks, own_hbm, old_ref, dif_ref, res, own_ref, old, enc, cand, recv, box, beside, edge, got_edge, corner,
            scl, scl_cand, scl_recv, scl_own, scl_got, dif, dif_edge, dif_beside, dif_got, dif_corner,
-           coef, slab, cur, wts, res, sem_in, sem_out, sem_dif_in,
+           coef, slab, cur, wts, sem_in, sem_dif_in,
            s_send, s_recv, r_send, r_recv, h_send, h_recv, d_send, d_recv, n_send, n_recv):
     species = dif_ref.shape[0]
     g, b = lax.axis_index("group"), lax.axis_index("box")
@@ -56,24 +63,35 @@
     sides = [(gs[0], b), (gs[1], b)]
     ends = [(g, bs[0]), (g, bs[1])]
     diagonal = [[(gs[i], bs[j]) for j in range(2)] for i in range(2)]
-    partners = ring[1:] + sides + ends + diagonal[0] + diagonal[1]
-
+    has_side = [g > 0, g < groups - 1]
+    has_end = [b < boxes - 1, b > 0]
+    around = [(sides[i], has_side[i]) for i in range(2)] + [(ends[j], has_end[j]) for j in range(2)]
+    around += [(diagonal[i][j], jnp.logical_and(has_side[i], has_end[j])) for i in range(2) for j in range(2)]
+
+    own_load = pltpu.make_async_copy(own_hbm, own_ref, sem_dif_in.at[1])
+    own_load.start()
     loads = []
     for k, (s0, n) in enumerate(chunks):
         cp = pltpu.make_async_copy(old_ref.at[:, pl.ds(s0, n)], old[k], sem_in.at[k])
         cp.start()
         loads.append(cp)
-    dif_load = pltpu.make_async_copy(dif_ref, dif, sem_dif_in)
+    dif_load = pltpu.make_async_copy(dif_ref, dif, sem_dif_in.at[0])
     dif_load.start()
 
     barrier = pltpu.get_barrier_semaphore()
-    for dev in partners:
+    for dev in ring[1:]:
         pl.semaphore_signal(barrier, inc=1, device_id=dev, device_id_type=MESH)
+    for dev, there in around:
+
+        @pl.when(there)
+        def _():
+            pl.semaphore_signal(barrier, inc=1, device_id=dev, device_id_type=MESH)
 
     def remote(src, dst, send, recv_sem, dev):
         return pltpu.make_async_remote_copy(src_ref=src, dst_ref=dst, send_sem=send, recv_sem=recv_sem,
                                             device_id=dev, device_id_type=MESH)
 
+    own_load.wait()
     slot = [own_ref[0, 1, base + lax.rem(x + d, BLOCK)] for d in range(BLOCK)]
     holder = own_ref[0, 0, b]
     came = lax.rem(lax.rem(holder, BLOCK) + BLOCK - x, BLOCK)
@@ -100,23 +118,35 @@
         scl_cand[d - 1] = scl[slot[d]]
     scl_recv[0] = scl[slot[0]]
 
-    pl.semaphore_wait(barrier, len(partners))
+    in_sides = has_side[0].astype(jnp.int32) + has_side[1].astype(jnp.int32)
+    in_ends = has_end[0].astype(jnp.int32) + has_end[1].astype(jnp.int32)
+    pl.semaphore_wait(barrier, BLOCK - 1 + in_sides + in_ends + in_sides * in_ends)
 
     sends = []
     waits = {}
 
-    def send(name, src, dst, send_sem, recv_sem, dev):
+    def send(name, src, dst, send_sem, recv_sem, dev, to=None, come=None):
         cp = remote(src, dst, send_sem, recv_sem, dev)
-        cp.start()
-        sends.append(cp)
-        waits.setdefault(name, []).append(cp)
+        when(to, cp.start)
+        sends.append((cp, to))
+        waits.setdefault(name, []).append((cp, come))
 
     def arrive(name):
-        for cp in waits.pop(name):
-            cp.wait_recv()
+        for cp, come in waits.pop(name):
+            when(come, cp.wait_recv)
+
+    def send_side(name, src, dst, send_sem, recv_sem, i):
+        send(name, src, dst, send_sem, recv_sem, sides[1 - i], has_side[1 - i], has_side[i])
+
+    def send_end(name, src, dst, send_sem, recv_sem, j):
+        send(name, src, dst, send_sem, recv_sem, ends[1 - j], has_end[1 - j], has_end[j])
+
+    def send_diagonal(name, src, dst, send_sem, recv_sem, i, j):
+        send(name, src, dst, send_sem, recv_sem, diagonal[1 - i][1 - j],
+             jnp.logical_and(has_side[1 - i], has_end[1 - j]), jnp.logical_and(has_side[i], has_end[j]))
 
     for e in range(2):
-        send("dif_edge", dif_edge.at[e], dif_got.at[e], d_send.at[e], d_recv.at[e], ends[1 - e])
+        send_end("dif_edge", dif_edge.at[e], dif_got.at[e], d_send.at[e], d_recv.at[e], e)
     for d in range(1, BLOCK):
         send("scl", scl_cand.at[d - 1], scl_recv.at[BLOCK - d], s_send.at[d - 1], s_recv.at[d - 1], ring[d])
 
@@ -139,20 +169,20 @@
             else:
                 recv[k][0] = enc[k][slot[0]]
     for i in range(2):
-        send("dif_side", dif, dif_beside.at[i], d_send.at[2 + i], d_recv.at[2 + i], sides[1 - i])
+        send_side("dif_side", dif, dif_beside.at[i], d_send.at[2 + i], d_recv.at[2 + i], i)
 
     arrive("scl")
     scl_own[...] = scl_recv[came]
     for i in range(2):
-        send("scl_all", scl_own, scl_got.at[i, 0], n_send.at[i], n_recv.at[i], sides[1 - i])
-        send("scl_all", scl_own, scl_got.at[2, 1 + i], n_send.at[2 + i], n_recv.at[2 + i], ends[1 - i])
+        send_side("scl_all", scl_own, scl_got.at[i, 0], n_send.at[i], n_recv.at[i], i)
+        send_end("scl_all", scl_own, scl_got.at[2, 1 + i], n_send.at[2 + i], n_recv.at[2 + i], i)
         for j in range(2):
             m = 4 + 2 * i + j
-            send("scl_all", scl_own, scl_got.at[i, 1 + j], n_send.at[m], n_recv.at[m], diagonal[1 - i][1 - j])
+            send_diagonal("scl_all", scl_own, scl_got.at[i, 1 + j], n_send.at[m], n_recv.at[m], i, j)
 
     arrive("dif_edge")
     for i in range(2):
-        send("dif_corner", dif_got, dif_corner.at[i], d_send.at[4 + i], d_recv.at[4 + i], sides[1 - i])
+        send_side("dif_corner", dif_got, dif_corner.at[i], d_send.at[4 + i], d_recv.at[4 + i], i)
 
     for k, (s0, n) in enumerate(chunks):
         arrive(("regrid", k))
@@ -167,17 +197,23 @@
 
         lax.fori_loop(0, n, choose, 0)
         for i in range(2):
-            send(("halo", k), box[k], beside[k].at[i], h_send.at[k, i], h_recv.at[k, i], sides[1 - i])
+            send_side(("halo", k), box[k], beside[k].at[i], h_send.at[k, i], h_recv.at[k, i], i)
         for e in range(2):
-            send(("halo", k), edge[k].at[e], got_edge[k].at[e], h_send.at[k, 2 + e], h_recv.at[k, 2 + e], ends[1 - e])
+            send_end(("halo", k), edge[k].at[e], got_edge[k].at[e], h_send.at[k, 2 + e], h_recv.at[k, 2 + e], e)
         for i in range(2):
             for e in range(2):
                 m = 4 + 2 * i + e
-                send(("halo", k), edge[k].at[e], corner[k].at[i, e], h_send.at[k, m], h_recv.at[k, m],
-                     diagonal[1 - i][1 - e])
-
-    in_side = [(g > 0).astype(jnp.float32), (g < groups - 1).astype(jnp.float32)]
-    in_end = [(b < boxes - 1).astype(jnp.float32), (b > 0).astype(jnp.float32)]
+                send_diagonal(("halo", k), edge[k].at[e], corner[k].at[i, e], h_send.at[k, m], h_recv.at[k, m], i, e)
+
+    in_side = [there.astype(jnp.float32) for there in has_side]
+    in_end = [there.astype(jnp.float32) for there in has_end]
+
+    def kept(there, value):
+        return jnp.where(there, value, 0.0)
+
+    def both(i, j):
+        return has_end[j] if i is None else jnp.logical_and(has_side[i], has_end[j])
+
     row = lax.broadcasted_iota(jnp.int32, (ZROWS, 128), 0)
     in_rows = jnp.where(row < 16, 1.0, jnp.where(row < 20, in_end[0], in_end[1]))
 
@@ -185,21 +221,14 @@
     arrive("dif_corner")
 
     def weigh(s, _):
-        for part in range(3):
+        for part, i in ((0, 0), (1, None), (2, 1)):
             for a in range(4):
-                rows = dif[s, a] if part == 1 else dif_beside[0 if part == 0 else 1, s, a]
-                rows = rows.astype(jnp.float32)
-                if part != 1:
-                    rows = rows * in_side[0 if part == 0 else 1]
-                coef[4 * part + a, 0:16] = rows
-            if part == 1:
-                after, before = dif_got[0, s], dif_got[1, s]
-                m = 1.0
-            else:
-                i = 0 if part == 0 else 1
-                after, before = dif_corner[i, 0, s], dif_corner[i, 1, s]
-                m = in_side[i]
-            halo = unpack_edges(after.astype(jnp.float32) * (in_end[0] * m), before.astype(jnp.float32) * (in_end[1] * m))
+                if i is None:
+                    coef[4 * part + a, 0:16] = dif[s, a].astype(jnp.float32)
+                else:
+                    coef[4 * part + a, 0:16] = kept(has_side[i], dif_beside[i, s, a].astype(jnp.float32))
+            tiles = [dif_got[j, s] if i is None else dif_corner[i, j, s] for j in range(2)]
+            halo = unpack_edges(*[kept(both(i, j), tiles[j].astype(jnp.float32)) for j in range(2)])
             for a in range(4):
                 coef[4 * part + a, 16:24] = halo[a]
         for a in range(1, 11):
@@ -222,27 +251,23 @@
     lax.fori_loop(0, species, weigh, 0)
     arrive("scl_all")
 
-    outs = []
     for k, (s0, n) in enumerate(chunks):
         arrive(("halo", k))
 
         def smooth(s, _):
             at = s0 + s
-            for part in range(3):
-                if part == 1:
-                    q, after, before = box[k][s], got_edge[k][0, s], got_edge[k][1, s]
-                    own_s, after_s, before_s = scl_own[pl.ds(at, 1)], scl_got[2, 1, pl.ds(at, 1)], scl_got[2, 2, pl.ds(at, 1)]
-                    m = 1.0
+            for part, i in ((0, 0), (1, None), (2, 1)):
+                if i is None:
+                    q = box[k][s].astype(jnp.int32).astype(jnp.float32) * scl_own[pl.ds(at, 1)]
+                    tiles = [got_edge[k][j, s] for j in range(2)]
+                    scales = [scl_got[2, 1 + j, pl.ds(at, 1)] for j in range(2)]
                 else:
-                    i = 0 if part == 0 else 1
-                    q, after, before = beside[k][i, s], corner[k][i, 0, s], corner[k][i, 1, s]
-                    own_s, after_s, before_s = (scl_got[i, j, pl.ds(at, 1)] for j in range(3))
-                    m = in_side[i]
-                    own_s = own_s * m
-                q = q.astype(jnp.int32).astype(jnp.float32) * own_s
-                after = after.astype(jnp.int32).astype(jnp.float32) * (after_s * (in_end[0] * m))
-                before = before.astype(jnp.int32).astype(jnp.float32) * (before_s * (in_end[1] * m))
-                halo = unpack_edges(after, before)
+                    q = beside[k][i, s].astype(jnp.int32).astype(jnp.float32)
+                    q = q * kept(has_side[i], scl_got[i, 0, pl.ds(at, 1)])
+                    tiles = [corner[k][i, j, s] for j in range(2)]
+                    scales = [scl_got[i, 1 + j, pl.ds(at, 1)] for j in range(2)]
+                halo = unpack_edges(*[tiles[j].astype(jnp.int32).astype(jnp.float32) * kept(both(i, j), scales[j])
+                                      for j in range(2)])
                 for a in range(4):
                     slab[4 * part + a, 0:16] = q[16 * a:16 * a + 16]
                     slab[4 * part + a, 16:24] = halo[a]
@@ -262,13 +287,8 @@
             return 0
 
         lax.fori_loop(0, n, smooth, 0)
-        cp = pltpu.make_async_copy(res.at[pl.ds(s0, n)], out_ref.at[pl.ds(s0, n)], sem_out.at[k])
-        cp.start()
-        outs.append(cp)
-    for cp in sends:
-        cp.wait_send()
-    for cp in outs:
-        cp.wait()
+    for cp, to in sends:
+        when(to, cp.wait_send)
 
 
 def cut(species):
@@ -290,6 +310,7 @@
     dma = pltpu.SemaphoreType.DMA
     nk = len(chunks)
     scratch = [
+        pltpu.SMEM(owners.shape, jnp.int32),
         [pltpu.VMEM((2, n, 4, 16, 128), f32) for _, n in chunks],
         [pltpu.VMEM((2, n, 64, 128), i16) for _, n in chunks],
         [pltpu.VMEM((3, n, 64, 128), i16) for _, n in chunks],
@@ -313,17 +334,18 @@
         pltpu.VMEM((12, ZROWS, 128), f32),
         pltpu.VMEM((2, 12, ZROWS, 128), f32),
         pltpu.VMEM((species, 10, 7, ZROWS, 128), f32),
-        pltpu.VMEM((species, 4, 16, 128), f32),
-        dma((nk,)), dma((nk,)), dma(()),
+        dma((nk,)), dma((2,)),
         dma((3,)), dma((3,)), dma((nk, 3)), dma((nk, 3)), dma((nk, 8)), dma((nk, 8)),
         dma((6,)), dma((6,)), dma((8,)), dma((8,)),
     ]
+    old_state, owners, diffusivity = (
+        pltpu.with_memory_space_constraint(v, pltpu.HBM) for v in (old_state, owners, diffusivity)
+    )
     return pl.pallas_call(
         functools.partial(kernel, chunks),
-        out_shape=jax.ShapeDtypeStruct(diffusivity.shape, f32),
-        in_specs=[pl.BlockSpec(memory_space=pltpu.SMEM), pl.BlockSpec(memory_space=pl.ANY),
-                  pl.BlockSpec(memory_space=pl.ANY)],
-        out_specs=pl.BlockSpec(memory_space=pl.ANY),
+        out_shape=pltpu.VMEM(diffusivity.shape, f32),
+        in_specs=[pl.BlockSpec(memory_space=pltpu.HBM)] * 3,
+        out_specs=pl.BlockSpec(memory_space=pltpu.VMEM),
         scratch_shapes=scratch,
         name="regrid_smooth",
         compiler_params=pltpu.CompilerParams(collective_id=0, has_side_effects=True, vmem_limit_bytes=40 * 2**20),

time: 38.9 us -> 25.3 us (0.65)
  the two profiles are of different devices: /device:TPU:1 before, /device:TPU:393 now
where the time goes in v2:
time: 25.3 us; the launch traced here: 25.2 us
  Pallas kernels  24.5 us (97%)
  local copies, waits for them, and re-layouts  0.72 us (3%)
    pallas_call x1, Pallas kernels, local(): pl.pallas_call(functools.partial(kernel, chunks), out_shape=pltpu.VMEM(di...  24.5 us
    unnamed x1, local copies, waits for them, and re-layouts  0.72 us

profile of v2, /device:TPU:393, one launch (start us, length us, event | category | flops | bytes accessed | tf_op | source)
XLA Modules:
  0.0 25.2 jit_solution(17280384502518419377)
XLA Ops:
  0.0 24.5 %regrid_smooth.1 = f32[9,4,16,128]{3,2,1,0:T(8,128)S(1)} custom-call(s32[1,2,64]{2,1,0:T(2,128)} %own_hbm.1, f32[2,9,4,16,128]{4,3,2,1,0:T(8,128)} %old_ref.1, bf16[9,4,16,128]{3,2,1,0:T(8,128)(2,1)} %dif_ref.1), custom_call_target="tpu_custom_call" | custom-call | tf_op jit(solution)/shard_map/regrid_smooth/pallas_call | solution.py:344
  24.5 0.7 %copy.5 = f32[9,4,16,128]{3,2,1,0:T(8,128)} copy(f32[9,4,16,128]{3,2,1,0:T(8,128)S(1)} %regrid_smooth.1) | data formatting | bytes 589824

commit v3 on v2

--- a/solution.py
+++ b/solution.py
@@ -48,10 +48,35 @@
     return out
 
 
-def kernel(chunks, own_hbm, old_ref, dif_ref, res, own_ref, old, enc, cand, recv, box, beside, edge, got_edge, corner,
+def pack_tips(first, last):
+    row = lax.broadcasted_iota(jnp.int32, (8, 128), 0)
+    f01, f23, l01, l23 = first[0:8], first[8:16], last[0:8], last[8:16]
+    return (
+        (jnp.where(row == 7, pltpu.roll(f01, 3, 0), f23), jnp.where(row == 3, pltpu.roll(f23, 3, 0), f01)),
+        (jnp.where(row == 4, pltpu.roll(l01, 5, 0), l23), jnp.where(row == 0, pltpu.roll(l23, 5, 0), l01)),
+    )
+
+
+def unpack_tips(side, n, p):
+    low = low_rows()
+    if side == 0:
+        return {
+            3: jnp.where(low, pltpu.roll(n, 4, 0), p),
+            2: jnp.where(low, n, pltpu.roll(p, 4, 0)),
+            1: jnp.where(low, pltpu.roll(n, 1, 0), pltpu.roll(p, 3, 0)),
+        }
+    return {
+        0: jnp.where(low, n, pltpu.roll(p, 4, 0)),
+        1: jnp.where(low, pltpu.roll(n, 4, 0), p),
+        2: jnp.where(low, pltpu.roll(n, 5, 0), pltpu.roll(p, 7, 0)),
+    }
+
+
+def kernel(chunks, own_hbm, old_ref, dif_ref, res, own_ref, old, enc, far, near, mix, merged, recv, box, beside, edge, got_edge, tips, tip,
+           corner, corner_f32,
            scl, scl_cand, scl_recv, scl_own, scl_got, dif, dif_edge, dif_beside, dif_got, dif_corner,
            coef, slab, cur, wts, sem_in, sem_dif_in,
-           s_send, s_recv, r_send, r_recv, h_send, h_recv, d_send, d_recv, n_send, n_recv):
+           s_send, s_recv, f_send, f_recv, r_send, r_recv, h_send, h_recv, d_send, d_recv, n_send, n_recv):
     species = dif_ref.shape[0]
     g, b = lax.axis_index("group"), lax.axis_index("box")
     groups, boxes = lax.axis_size("group"), lax.axis_size("box")
@@ -95,16 +120,9 @@
     slot = [own_ref[0, 1, base + lax.rem(x + d, BLOCK)] for d in range(BLOCK)]
     holder = own_ref[0, 0, b]
     came = lax.rem(lax.rem(holder, BLOCK) + BLOCK - x, BLOCK)
-
-    dif_load.wait()
-
-    def dif_pack(s, _):
-        first, last = pack_edges([dif[s, a].astype(jnp.float32) for a in range(4)])
-        dif_edge[0, s] = first.astype(jnp.bfloat16)
-        dif_edge[1, s] = last.astype(jnp.bfloat16)
-        return 0
-
-    lax.fori_loop(0, species, dif_pack, 0)
+    left, right = lax.rem(x + BLOCK - 1, BLOCK), lax.rem(x + 1, BLOCK)
+    behind = (lax.rem(own_ref[0, 0, base + left], BLOCK) == right, lax.rem(own_ref[0, 0, base + right], BLOCK) == left)
+    place = [jnp.where(came == 0, 0, jnp.where(came == (3, 1)[h], 2, 1)) for h in range(2)]
 
     for cp in loads:
         cp.wait()
@@ -118,6 +136,24 @@
         scl_cand[d - 1] = scl[slot[d]]
     scl_recv[0] = scl[slot[0]]
 
+    for k, (s0, n) in enumerate(chunks):
+
+        def encode(s, _):
+            for t in range(2):
+                inv = 1.0 / scl[t, pl.ds(s0 + s, 1)]
+                for a in range(4):
+                    q = jnp.round(old[k][t, s, a] * inv).astype(jnp.int32)
+                    enc[k][t, a // 2, s, pl.ds(16 * (a % 2), 16)] = q.astype(jnp.int16)
+            return 0
+
+        lax.fori_loop(0, n, encode, 0)
+        for h in range(2):
+            far[k][h] = enc[k][slot[2], h]
+            near[k][h] = enc[k][slot[(1, 3)[h]], h]
+            mix[k][h][1] = enc[k][slot[(3, 1)[h]], h]
+            recv[k][h][0] = enc[k][slot[0], h]
+    dif_load.wait()
+
     in_sides = has_side[0].astype(jnp.int32) + has_side[1].astype(jnp.int32)
     in_ends = has_end[0].astype(jnp.int32) + has_end[1].astype(jnp.int32)
     pl.semaphore_wait(barrier, BLOCK - 1 + in_sides + in_ends + in_sides * in_ends)
@@ -145,31 +181,36 @@
         send(name, src, dst, send_sem, recv_sem, diagonal[1 - i][1 - j],
              jnp.logical_and(has_side[1 - i], has_end[1 - j]), jnp.logical_and(has_side[i], has_end[j]))
 
+    for k in range(len(chunks)):
+        for h in range(2):
+            send(("far", k), far[k].at[h], mix[k][h].at[0], f_send.at[k, h], f_recv.at[k, h], ring[(BLOCK - 1, 1)[h]])
+    for d in range(1, BLOCK):
+        send("scl", scl_cand.at[d - 1], scl_recv.at[BLOCK - d], s_send.at[d - 1], s_recv.at[d - 1], ring[d])
+    for k in range(len(chunks)):
+        for h in range(2):
+            send(("regrid", k), near[k].at[h], recv[k][h].at[2], r_send.at[k, h], r_recv.at[k, h],
+                 ring[(1, BLOCK - 1)[h]])
+    for i in range(2):
+        send_side("dif_side", dif, dif_beside.at[i], d_send.at[2 + i], d_recv.at[2 + i], i)
+
+
+    def dif_pack(s, _):
+        first, last = pack_edges([dif[s, a].astype(jnp.float32) for a in range(4)])
+        dif_edge[0, s] = first.astype(jnp.bfloat16)
+        dif_edge[1, s] = last.astype(jnp.bfloat16)
+        return 0
+
+    lax.fori_loop(0, species, dif_pack, 0)
+
     for e in range(2):
         send_end("dif_edge", dif_edge.at[e], dif_got.at[e], d_send.at[e], d_recv.at[e], e)
-    for d in range(1, BLOCK):
-        send("scl", scl_cand.at[d - 1], scl_recv.at[BLOCK - d], s_send.at[d - 1], s_recv.at[d - 1], ring[d])
-
-    for k, (s0, n) in enumerate(chunks):
-
-        def encode(s, _):
-            for t in range(2):
-                inv = 1.0 / scl[t, pl.ds(s0 + s, 1)]
-                for a in range(4):
-                    q = jnp.round(old[k][t, s, a] * inv).astype(jnp.int32)
-                    enc[k][t, s, pl.ds(16 * a, 16)] = q.astype(jnp.int16)
-            return 0
-
-        lax.fori_loop(0, n, encode, 0)
-        for d in range(BLOCK):
-            if d:
-                cand[k][d - 1] = enc[k][slot[d]]
-                send(("regrid", k), cand[k].at[d - 1], recv[k].at[BLOCK - d], r_send.at[k, d - 1], r_recv.at[k, d - 1],
-                     ring[d])
-            else:
-                recv[k][0] = enc[k][slot[0]]
-    for i in range(2):
-        send_side("dif_side", dif, dif_beside.at[i], d_send.at[2 + i], d_recv.at[2 + i], i)
+
+    for k in range(len(chunks)):
+        arrive(("far", k))
+        for h in range(2):
+            merged[k][h] = mix[k][h][jnp.where(behind[h], 0, 1)]
+            send(("regrid", k), merged[k].at[h], recv[k][h].at[1], r_send.at[k, 2 + h], r_recv.at[k, 2 + h],
+                 ring[(BLOCK - 1, 1)[h]])
 
     arrive("scl")
     scl_own[...] = scl_recv[came]
@@ -188,14 +229,27 @@
         arrive(("regrid", k))
 
         def choose(s, _):
-            q = recv[k][came, s]
-            box[k][s] = q
-            first, last = pack_edges([q[16 * a:16 * a + 16].astype(jnp.int32) for a in range(4)])
+            layers = []
+            for h in range(2):
+                q = recv[k][h][place[h], s]
+                box[k][s, pl.ds(32 * h, 32)] = q
+                q = q.astype(jnp.int32)
+                layers += [q[0:16], q[16:32]]
+            first, last = pack_edges(layers)
             edge[k][0, s] = first.astype(jnp.int16)
             edge[k][1, s] = last.astype(jnp.int16)
+            tip_rows = pack_tips(first, last)
+            for e in range(2):
+                for i in range(2):
+                    tips[k][i, e, s] = tip_rows[e][i]
             return 0
 
         lax.fori_loop(0, n, choose, 0)
+        for i in range(2):
+            for e in range(2):
+                for m in range(tip[k].shape[2]):
+                    pair = tips[k][i, e, pl.ds(2 * m, 2)].reshape(16, 128)
+                    tip[k][i, e, m] = pair.astype(jnp.int16)
         for i in range(2):
             send_side(("halo", k), box[k], beside[k].at[i], h_send.at[k, i], h_recv.at[k, i], i)
         for e in range(2):
@@ -203,7 +257,7 @@
         for i in range(2):
             for e in range(2):
                 m = 4 + 2 * i + e
-                send_diagonal(("halo", k), edge[k].at[e], corner[k].at[i, e], h_send.at[k, m], h_recv.at[k, m], i, e)
+                send_diagonal(("halo", k), tip[k].at[i, e], corner[k].at[i, e], h_send.at[k, m], h_recv.at[k, m], i, e)
 
     in_side = [there.astype(jnp.float32) for there in has_side]
     in_end = [there.astype(jnp.float32) for there in has_end]
@@ -253,24 +307,29 @@
 
     for k, (s0, n) in enumerate(chunks):
         arrive(("halo", k))
+        for i in range(2):
+            for e in range(2):
+                for m in range(tip[k].shape[2]):
+                    pair = corner[k][i, e, m].astype(jnp.int32).astype(jnp.float32)
+                    corner_f32[i, e, pl.ds(2 * m, 2)] = pair.reshape(2, 8, 128)
 
         def smooth(s, _):
             at = s0 + s
             for part, i in ((0, 0), (1, None), (2, 1)):
                 if i is None:
                     q = box[k][s].astype(jnp.int32).astype(jnp.float32) * scl_own[pl.ds(at, 1)]
-                    tiles = [got_edge[k][j, s] for j in range(2)]
-                    scales = [scl_got[2, 1 + j, pl.ds(at, 1)] for j in range(2)]
+                    halo = dict(enumerate(unpack_edges(*[
+                        got_edge[k][j, s].astype(jnp.int32).astype(jnp.float32)
+                        * kept(has_end[j], scl_got[2, 1 + j, pl.ds(at, 1)]) for j in range(2)])))
                 else:
                     q = beside[k][i, s].astype(jnp.int32).astype(jnp.float32)
                     q = q * kept(has_side[i], scl_got[i, 0, pl.ds(at, 1)])
-                    tiles = [corner[k][i, j, s] for j in range(2)]
-                    scales = [scl_got[i, 1 + j, pl.ds(at, 1)] for j in range(2)]
-                halo = unpack_edges(*[tiles[j].astype(jnp.int32).astype(jnp.float32) * kept(both(i, j), scales[j])
-                                      for j in range(2)])
+                    halo = unpack_tips(i, *[corner_f32[i, j, s] * kept(both(i, j), scl_got[i, 1 + j, pl.ds(at, 1)])
+                                            for j in range(2)])
                 for a in range(4):
                     slab[4 * part + a, 0:16] = q[16 * a:16 * a + 16]
-                    slab[4 * part + a, 16:24] = halo[a]
+                    if a in halo:
+                        slab[4 * part + a, 16:24] = halo[a]
             for it in range(ITERS):
                 src = slab if it == 0 else cur.at[(it - 1) % 2]
                 for a in range(1 + it, 11 - it):
@@ -312,14 +371,20 @@
     scratch = [
         pltpu.SMEM(owners.shape, jnp.int32),
         [pltpu.VMEM((2, n, 4, 16, 128), f32) for _, n in chunks],
-        [pltpu.VMEM((2, n, 64, 128), i16) for _, n in chunks],
-        [pltpu.VMEM((3, n, 64, 128), i16) for _, n in chunks],
-        [pltpu.VMEM((4, n, 64, 128), i16) for _, n in chunks],
+        [pltpu.VMEM((2, 2, n, 32, 128), i16) for _, n in chunks],
+        [pltpu.VMEM((2, n, 32, 128), i16) for _, n in chunks],
+        [pltpu.VMEM((2, n, 32, 128), i16) for _, n in chunks],
+        [[pltpu.VMEM((2, n, 32, 128), i16) for _ in range(2)] for _, n in chunks],
+        [pltpu.VMEM((2, n, 32, 128), i16) for _, n in chunks],
+        [[pltpu.VMEM((3, n, 32, 128), i16) for _ in range(2)] for _, n in chunks],
         [pltpu.VMEM((n, 64, 128), i16) for _, n in chunks],
         [pltpu.VMEM((2, n, 64, 128), i16) for _, n in chunks],
         [pltpu.VMEM((2, n, 16, 128), i16) for _, n in chunks],
         [pltpu.VMEM((2, n, 16, 128), i16) for _, n in chunks],
-        [pltpu.VMEM((2, 2, n, 16, 128), i16) for _, n in chunks],
+        [pltpu.VMEM((2, 2, n + n % 2, 8, 128), jnp.int32) for _, n in chunks],
+        [pltpu.VMEM((2, 2, (n + 1) // 2, 16, 128), i16) for _, n in chunks],
+        [pltpu.VMEM((2, 2, (n + 1) // 2, 16, 128), i16) for _, n in chunks],
+        pltpu.VMEM((2, 2, max(n for _, n in chunks) + 1, 8, 128), f32),
         pltpu.VMEM((2, species, 128), f32),
         pltpu.VMEM((3, species, 128), f32),
         pltpu.VMEM((4, species, 128), f32),
@@ -335,7 +400,7 @@
         pltpu.VMEM((2, 12, ZROWS, 128), f32),
         pltpu.VMEM((species, 10, 7, ZROWS, 128), f32),
         dma((nk,)), dma((2,)),
-        dma((3,)), dma((3,)), dma((nk, 3)), dma((nk, 3)), dma((nk, 8)), dma((nk, 8)),
+        dma((3,)), dma((3,)), dma((nk, 2)), dma((nk, 2)), dma((nk, 4)), dma((nk, 4)), dma((nk, 8)), dma((nk, 8)),
         dma((6,)), dma((6,)), dma((8,)), dma((8,)),
     ]
     old_state, owners, diffusivity = (

time: 25.3 us -> 23.4 us (0.925)
  Pallas kernels: 24.5 us -> 22.6 us
    pallas_call x1, Pallas kernels: 24.5 us -> 22.6 us  [local(): pl.pallas_call(functools.partial(kernel, chunks), out_shape=pltpu.VMEM(di...]
where the time goes in v3:
time: 23.4 us; the launch traced here: 23.3 us
  Pallas kernels  22.6 us (97%)
  local copies, waits for them, and re-layouts  0.72 us (3%)
    pallas_call x1, Pallas kernels, local(): pl.pallas_call(functools.partial(kernel, chunks), out_shape=pltpu.VMEM(di...  22.6 us
    unnamed x1, local copies, waits for them, and re-layouts  0.72 us

profile of v3, /device:TPU:393, one launch (start us, length us, event | category | flops | bytes accessed | tf_op | source)
XLA Modules:
  0.0 23.3 jit_solution(5285108970754351937)
XLA Ops:
  0.0 22.6 %regrid_smooth.1 = f32[9,4,16,128]{3,2,1,0:T(8,128)S(1)} custom-call(s32[1,2,64]{2,1,0:T(2,128)} %own_hbm.1, f32[2,9,4,16,128]{4,3,2,1,0:T(8,128)} %old_ref.1, bf16[9,4,16,128]{3,2,1,0:T(8,128)(2,1)} %dif_ref.1), custom_call_target="tpu_custom_call" | custom-call | tf_op jit(solution)/shard_map/regrid_smooth/pallas_call | solution.py:409
  22.6 0.7 %copy.5 = f32[9,4,16,128]{3,2,1,0:T(8,128)} copy(f32[9,4,16,128]{3,2,1,0:T(8,128)S(1)} %regrid_smooth.1) | data formatting | bytes 589824

commit v4 on v0

v4 whole, which is shorter than its diff:
```python
import jax
import jax.numpy as jnp
from jax import lax
from jax.experimental import pallas as pl
from jax.experimental.pallas import tpu as pltpu
from jax.sharding import PartitionSpec as P

MESH = pl.DeviceIdType.MESH
BLOCK = 4
ITERS = 4
LEVELS = 32767.0
ZROWS = 24


def when(condition, act):
    if condition is None:
        act()
    else:
        pl.when(condition)(act)


def low_rows():
    return lax.broadcasted_iota(jnp.int32, (8, 128), 0) < 4


def pack_edges(rows):
    low = low_rows()
    first, last = [], []
    for a in (0, 2):
        p, q = rows[a], rows[a + 1]
        first.append(jnp.where(low, p[0:8], pltpu.roll(q[0:8], 4, 0)))
        last.append(jnp.where(low, pltpu.roll(p[8:16], 4, 0), q[8:16]))
    return jnp.concatenate(first, 0), jnp.concatenate(last, 0)


def unpack_edges(after, before):
    low = low_rows()
    out = []
    for a in range(4):
        n = after[8 * (a // 2):8 * (a // 2) + 8]
        p = before[8 * (a // 2):8 * (a // 2) + 8]
        if a % 2 == 0:
            out.append(jnp.where(low, n, pltpu.roll(p, 4, 0)))
        else:
            out.append(jnp.where(low, pltpu.roll(n, 4, 0), p))
    return out


def pack_tips(first, last):
    row = lax.broadcasted_iota(jnp.int32, (8, 128), 0)
    f01, f23, l01, l23 = first[0:8], first[8:16], last[0:8], last[8:16]
    return (
        (jnp.where(row == 7, pltpu.roll(f01, 3, 0), f23), jnp.where(row == 3, pltpu.roll(f23, 3, 0), f01)),
        (jnp.where(row == 4, pltpu.roll(l01, 5, 0), l23), jnp.where(row == 0, pltpu.roll(l23, 5, 0), l01)),
    )


def unpack_tips(side, n, p):
    low = low_rows()
    if side == 0:
        return {
            3: jnp.where(low, pltpu.roll(n, 4, 0), p),
            2: jnp.where(low, n, pltpu.roll(p, 4, 0)),
            1: jnp.where(low, pltpu.roll(n, 1, 0), pltpu.roll(p, 3, 0)),
        }
    return {
        0: jnp.where(low, n, pltpu.roll(p, 4, 0)),
        1: jnp.where(low, pltpu.roll(n, 4, 0), p),
        2: jnp.where(low, pltpu.roll(n, 5, 0), pltpu.roll(p, 7, 0)),
    }


def kernel(own_hbm, old_ref, dif_ref, res, own_ref, old, far, via, near, mine, merged, got, kept_own, box, beside,
           edge, got_edge, tips, tip, corner, corner_f32, scl_cand, scl_recv, scl_own, scl_got,
           dif, dif_edge, dif_beside, dif_got, dif_corner, coef, slab, cur, wts, pool,
           sem_in, sem_out, sem_far, sem_regrid, sem_halo, sem_scl, sem_dif):
    species = dif_ref.shape[0]
    count, size, pairs = tip.shape[0], slab.shape[0], tip.shape[3]
    g, b = lax.axis_index("group"), lax.axis_index("box")
    groups, boxes = lax.axis_size("group"), lax.axis_size("box")
    x = lax.rem(b, BLOCK)
    base = b - x
    ring = [None] + [(g, base + lax.rem(x + d, BLOCK)) for d in range(1, BLOCK)]
    gs = (lax.rem(g + groups - 1, groups), lax.rem(g + 1, groups))
    bs = (lax.rem(b + 1, boxes), lax.rem(b + boxes - 1, boxes))
    sides = [(gs[0], b), (gs[1], b)]
    ends = [(g, bs[0]), (g, bs[1])]
    diagonal = [[(gs[i], bs[j]) for j in range(2)] for i in range(2)]
    has_side = [g > 0, g < groups - 1]
    has_end = [b < boxes - 1, b > 0]

    def both(i, j):
        return has_end[j] if i is None else jnp.logical_and(has_side[i], has_end[j])

    around = [(sides[i], has_side[i]) for i in range(2)] + [(ends[j], has_end[j]) for j in range(2)]
    around += [(diagonal[i][j], both(i, j)) for i in range(2) for j in range(2)]

    barrier = pltpu.get_barrier_semaphore()
    for dev in ring[1:]:
        pl.semaphore_signal(barrier, inc=1, device_id=dev, device_id_type=MESH)
    for dev, there in around:

        @pl.when(there)
        def _():
            pl.semaphore_signal(barrier, inc=1, device_id=dev, device_id_type=MESH)

    old_load = pltpu.make_async_copy(old_ref, old, sem_in.at[0])
    old_load.start()
    own_load = pltpu.make_async_copy(own_hbm, own_ref, sem_in.at[1])
    own_load.start()
    dif_load = pltpu.make_async_copy(dif_ref, dif, sem_in.at[2])
    dif_load.start()

    def message(src, dst, recv_sem, dev, to=None):
        cp = pltpu.make_async_remote_copy(src_ref=src, dst_ref=dst, send_sem=sem_out, recv_sem=recv_sem,
                                          device_id=dev, device_id_type=MESH)
        return cp, to

    def to_side(src, dst, recv_sem, i):
        return message(src, dst, recv_sem, sides[1 - i], has_side[1 - i])

    def to_end(src, dst, recv_sem, j):
        return message(src, dst, recv_sem, ends[1 - j], has_end[1 - j])

    def to_diagonal(src, dst, recv_sem, i, j):
        return message(src, dst, recv_sem, diagonal[1 - i][1 - j], both(1 - i, 1 - j))

    def start(messages):
        for cp, to in messages:
            when(to, cp.start)

    def wait_units(sem, units):
        span = pool.at[pl.ds(0, 8 * units)]
        pltpu.make_async_copy(span, span, sem).wait()

    in_sides = has_side[0].astype(jnp.int32) + has_side[1].astype(jnp.int32)
    in_ends = has_end[0].astype(jnp.int32) + has_end[1].astype(jnp.int32)

    def wait_around(sem, units):
        for ns in (1, 2):
            for ne in (1, 2):

                @pl.when(jnp.logical_and(in_sides == ns, in_ends == ne))
                def _():
                    wait_units(sem, units(ns, ne))

    scl_units = scl_own.shape[0] // 8

    def halo_units(ns, ne):
        return ne * size + ns * ne * pairs + ns * 4 * size

    def all_units(ns, ne):
        fixed = 3 * 4 * species + 3 * scl_units
        around = scl_units * (ns + ne + ns * ne) + species * (6 * ns + ne)
        return fixed + around + count * halo_units(ns, ne)

    def part(k):
        return pl.ds(k * size, size)

    ahead = (ring[BLOCK - 1], ring[1])

    def far_messages(k):
        return [message(far.at[h, part(k)], via.at[h, part(k)], sem_far.at[k], ahead[h]) for h in range(2)]

    def near_messages(k):
        return [message(near.at[h, part(k)], got.at[1, h, part(k)], sem_regrid.at[k], ahead[1 - h]) for h in range(2)]

    def merged_messages(k):
        return [message(merged.at[h, part(k)], got.at[0, h, part(k)], sem_regrid.at[k], ahead[h]) for h in range(2)]

    def halo_messages(k):
        out = [to_end(edge.at[e, part(k)], got_edge.at[e, part(k)], sem_halo.at[k], e) for e in range(2)]
        out += [to_diagonal(tip.at[k, i, e], corner.at[k, i, e], sem_halo.at[k], i, e)
                for i in range(2) for e in range(2)]
        return out + [to_side(box.at[part(k)], beside.at[i, part(k)], sem_halo.at[k], i) for i in range(2)]

    scl_messages = [message(scl_cand.at[d - 1], scl_recv.at[BLOCK - d], sem_scl.at[0], ring[d]) for d in range(1, BLOCK)]
    scl_around = [to_side(scl_own, scl_got.at[i, 0], sem_scl.at[1], i) for i in range(2)]
    scl_around += [to_end(scl_own, scl_got.at[2, 1 + j], sem_scl.at[1], j) for j in range(2)]
    scl_around += [to_diagonal(scl_own, scl_got.at[i, 1 + j], sem_scl.at[1], i, j) for i in range(2) for j in range(2)]
    dif_ends = [to_end(dif_edge.at[e], dif_got.at[e], sem_dif.at[0], e) for e in range(2)]
    dif_sides = [to_side(dif, dif_beside.at[i], sem_dif.at[1], i) for i in range(2)]
    dif_corners = [to_side(dif_got, dif_corner.at[i], sem_dif.at[1], i) for i in range(2)]

    def each(n, act):
        def body(k, _):
            act(k)
            return 0

        lax.fori_loop(0, n, body, 0)

    own_load.wait()
    first_slot = [own_ref[0, 1, base + lax.rem(x + d, BLOCK)] == 0 for d in range(BLOCK)]
    holder = own_ref[0, 0, b]
    came = lax.rem(lax.rem(holder, BLOCK) + BLOCK - x, BLOCK)
    left, right = lax.rem(x + BLOCK - 1, BLOCK), lax.rem(x + 1, BLOCK)
    behind = (lax.rem(own_ref[0, 0, base + left], BLOCK) == right, lax.rem(own_ref[0, 0, base + right], BLOCK) == left)
    old_load.wait()

    def encode(s):
        codes, scales = [], []
        for t in range(2):
            layers = [old[t, s, a] for a in range(4)]
            m = jnp.maximum(jnp.maximum(jnp.abs(layers[0]), jnp.abs(layers[1])),
                            jnp.maximum(jnp.abs(layers[2]), jnp.abs(layers[3])))
            m = jnp.maximum(jnp.max(m, axis=0, keepdims=True), 1e-30)
            scale = m * (1.0 / LEVELS)
            inv = 1.0 / scale
            rows = [jnp.round(v * inv).astype(jnp.int32) for v in layers]
            codes.append([jnp.concatenate(rows[2 * h:2 * h + 2], 0) for h in range(2)])
            scales.append(scale)

        def code(d, h):
            return jnp.where(first_slot[d], codes[0][h], codes[1][h]).astype(jnp.int16)

        for h in range(2):
            far[h, s] = code(2, h)
            near[h, s] = code((1, 3)[h], h)
            mine[h, s] = code((3, 1)[h], h)
            kept_own[h, s] = code(0, h)
        for d in range(BLOCK):
            scale = jnp.where(first_slot[d], scales[0], scales[1])
            if d:
                scl_cand[d - 1, pl.ds(s, 1)] = scale
            else:
                scl_recv[0, pl.ds(s, 1)] = scale

    each(species, encode)
    dif_load.wait()

    pl.semaphore_wait(barrier, BLOCK - 1 + in_sides + in_ends + in_sides * in_ends)

    each(count, lambda k: start(far_messages(k)))
    start(scl_messages)
    each(count, lambda k: start(near_messages(k)))
    start(dif_sides)

    def dif_pack(s):
        first, last = pack_edges([dif[s, a].astype(jnp.float32) for a in range(4)])
        dif_edge[0, s] = first.astype(jnp.bfloat16)
        dif_edge[1, s] = last.astype(jnp.bfloat16)

    each(species, dif_pack)
    start(dif_ends)

    def merge(k):
        wait_units(sem_far.at[k], 4 * size)
        for q in range(size):
            for h in range(2):
                s = k * size + q
                merged[h, s] = jnp.where(behind[h], via[h, s], mine[h, s])
        start(merged_messages(k))

    each(count, merge)

    wait_units(sem_scl.at[0], 3 * scl_units)
    scl_own[...] = scl_recv[came]
    start(scl_around)
    wait_around(sem_dif.at[0], lambda ns, ne: species * ne)
    start(dif_corners)

    def choose(k):
        wait_units(sem_regrid.at[k], 8 * size)
        for c in range(size):
            s = k * size + c
            layers = []
            for h in range(2):
                q = jnp.where(came == 0, kept_own[h, s], jnp.where(came == (3, 1)[h], got[1, h, s], got[0, h, s]))
                box[s, pl.ds(32 * h, 32)] = q
                q = q.astype(jnp.int32)
                layers += [q[0:16], q[16:32]]
            first, last = pack_edges(layers)
            edge[0, s] = first.astype(jnp.int16)
            edge[1, s] = last.astype(jnp.int16)
            tip_rows = pack_tips(first, last)
            for e in range(2):
                for i in range(2):
                    tips[i, e, c] = tip_rows[e][i]
        for i in range(2):
            for e in range(2):
                for m in range(tip.shape[3]):
                    pair = tips[i, e, pl.ds(2 * m, 2)].reshape(16, 128)
                    tip[k, i, e, m] = pair.astype(jnp.int16)
        start(halo_messages(k))

    each(count, choose)

    in_side = [there.astype(jnp.float32) for there in has_side]
    in_end = [there.astype(jnp.float32) for there in has_end]

    def kept(there, value):
        return jnp.where(there, value, 0.0)

    row = lax.broadcasted_iota(jnp.int32, (ZROWS, 128), 0)
    in_rows = jnp.where(row < 16, 1.0, jnp.where(row < 20, in_end[0], in_end[1]))

    wait_around(sem_dif.at[1], lambda ns, ne: 6 * species * ns)

    def weigh(at):
        for block, i in ((0, 0), (1, None), (2, 1)):
            for a in range(4):
                if i is None:
                    coef[4 * block + a, 0:16] = dif[at, a].astype(jnp.float32)
                else:
                    coef[4 * block + a, 0:16] = kept(has_side[i], dif_beside[i, at, a].astype(jnp.float32))
            tiles = [dif_got[j, at] if i is None else dif_corner[i, j, at] for j in range(2)]
            halo = unpack_edges(*[kept(both(i, j), tiles[j].astype(jnp.float32)) for j in range(2)])
            for a in range(4):
                coef[4 * block + a, 16:24] = halo[a]
        c = coef[0]
        from_layer = None
        for a in range(11):
            above = coef[a + 1]
            to_layer = 0.25 * (c + above)
            wts[at, a, 0] = to_layer
            if a:
                to_row = 0.25 * (c + pltpu.roll(c, ZROWS - 1, 0))
                to_column = 0.25 * (c + pltpu.roll(c, 127, 1))
                total = (to_layer + from_layer) + (to_row + pltpu.roll(to_row, 1, 0))
                total = total + (to_column + pltpu.roll(to_column, 1, 1))
                inverse = in_rows / (1.0 + total)
                if a < 4:
                    inverse = inverse * in_side[0]
                elif a > 7:
                    inverse = inverse * in_side[1]
                wts[at, a, 1] = to_row
                wts[at, a, 2] = to_column
                wts[at, a, 3] = inverse
            from_layer, c = to_layer, above

    each(species, weigh)

    wait_around(sem_scl.at[1], lambda ns, ne: scl_units * (ns + ne + ns * ne))

    def smooth(k):
        wait_around(sem_halo.at[k], halo_units)
        for i in range(2):
            for e in range(2):
                for m in range(tip.shape[3]):
                    pair = corner[k, i, e, m].astype(jnp.int32).astype(jnp.float32)
                    corner_f32[i, e, pl.ds(2 * m, 2)] = pair.reshape(2, 8, 128)
        for s in range(size):
            at = k * size + s
            for block, i in ((0, 0), (1, None), (2, 1)):
                if i is None:
                    q = box[at].astype(jnp.int32).astype(jnp.float32) * scl_own[pl.ds(at, 1)]
                    halo = dict(enumerate(unpack_edges(*[
                        got_edge[j, at].astype(jnp.int32).astype(jnp.float32)
                        * kept(has_end[j], scl_got[2, 1 + j, pl.ds(at, 1)]) for j in range(2)])))
                else:
                    q = beside[i, at].astype(jnp.int32).astype(jnp.float32)
                    q = q * kept(has_side[i], scl_got[i, 0, pl.ds(at, 1)])
                    halo = unpack_tips(i, *[corner_f32[i, j, s] * kept(both(i, j), scl_got[i, 1 + j, pl.ds(at, 1)])
                                            for j in range(2)])
                for a in range(4):
                    slab[s, 4 * block + a, 0:16] = q[16 * a:16 * a + 16]
                    if a in halo:
                        slab[s, 4 * block + a, 16:24] = halo[a]
        for it in range(ITERS):
            for s in range(size):
                at = k * size + s
                src = slab.at[s] if it == 0 else cur.at[(it - 1) % 2, s]
                below, v = src[it], src[it + 1]
                from_layer = wts[at, it, 0]
                for a in range(1 + it, 11 - it):
                    rows = 16 if it == ITERS - 1 or a in (1 + it, 10 - it) else ZROWS
                    above = src[a + 1]
                    to_layer, to_row, to_column, inverse = (wts[at, a, f] for f in range(4))
                    acc = slab[s, a] + from_layer * below + to_layer * above
                    acc = acc + (pltpu.roll(to_row * v, 1, 0) + to_row * pltpu.roll(v, ZROWS - 1, 0))
                    v_rows, to_rows = v[0:rows], to_column[0:rows]
                    acc = acc[0:rows] + (pltpu.roll(to_rows * v_rows, 1, 1) + to_rows * pltpu.roll(v_rows, 127, 1))
                    acc = acc * inverse[0:rows]
                    if it == ITERS - 1:
                        res[at, a - 4] = acc
                    else:
                        cur[it % 2, s, a, 0:rows] = acc
                    from_layer, below, v = to_layer, v, above

    each(count, smooth)
    wait_around(sem_out, all_units)


def local(old_state, owners, diffusivity):
    species = diffusivity.shape[0]
    size = 3 if species % 3 == 0 else 1
    count = species // size
    pairs, padded = (size + 1) // 2, (species + 7) // 8 * 8
    units = 18 * species + 3 * padded // 8 + padded + 14 * species + count * (10 * size + 4 * pairs)
    i16, i32, bf16, f32 = jnp.int16, jnp.int32, jnp.bfloat16, jnp.float32
    dma = pltpu.SemaphoreType.DMA
    halves = pltpu.VMEM((2, species, 32, 128), i16)
    scratch = [
        pltpu.SMEM(owners.shape, i32),
        pltpu.VMEM(old_state.shape, f32),
        halves, halves, halves, halves, halves,
        pltpu.VMEM((2, 2, species, 32, 128), i16),
        halves,
        pltpu.VMEM((species, 64, 128), i16),
        pltpu.VMEM((2, species, 64, 128), i16),
        pltpu.VMEM((2, species, 16, 128), i16),
        pltpu.VMEM((2, species, 16, 128), i16),
        pltpu.VMEM((2, 2, 2 * pairs, 8, 128), i32),
        pltpu.VMEM((count, 2, 2, pairs, 16, 128), i16),
        pltpu.VMEM((count, 2, 2, pairs, 16, 128), i16),
        pltpu.VMEM((2, 2, 2 * pairs, 8, 128), f32),
        pltpu.VMEM((3, padded, 128), f32),
        pltpu.VMEM((4, padded, 128), f32),
        pltpu.VMEM((padded, 128), f32),
        pltpu.VMEM((3, 3, padded, 128), f32),
        pltpu.VMEM((species, 4, 16, 128), bf16),
        pltpu.VMEM((2, species, 16, 128), bf16),
        pltpu.VMEM((2, species, 4, 16, 128), bf16),
        pltpu.VMEM((2, species, 16, 128), bf16),
        pltpu.VMEM((2, 2, species, 16, 128), bf16),
        pltpu.VMEM((12, ZROWS, 128), f32),
        pltpu.VMEM((size, 12, ZROWS, 128), f32),
        pltpu.VMEM((2, size, 12, ZROWS, 128), f32),
        pltpu.VMEM((species, 11, 4, ZROWS, 128), f32),
        pltpu.VMEM((8 * units, 128), f32),
        dma((3,)), dma(()), dma((count,)), dma((count,)), dma((count,)), dma((2,)), dma((2,)),
    ]
    old_state, owners, diffusivity = (
        pltpu.with_memory_space_constraint(v, pltpu.HBM) for v in (old_state, owners, diffusivity)
    )
    return pl.pallas_call(
        kernel,
        out_shape=pltpu.VMEM(diffusivity.shape, f32),
        in_specs=[pl.BlockSpec(memory_space=pltpu.HBM)] * 3,
        out_specs=pl.BlockSpec(memory_space=pltpu.VMEM),
        scratch_shapes=scratch,
        name="regrid_smooth",
        compiler_params=pltpu.CompilerParams(collective_id=0, has_side_effects=True, vmem_limit_bytes=40 * 2**20),
    )(owners, old_state, diffusivity)


def solution(mesh):
    placed = (
        P(None, None, "group", "box", None),
        P("group", None, None),
        P(None, "group", "box", None),
    )
    return jax.shard_map(
        local, mesh=mesh, in_specs=placed, out_specs=P(None, "group", "box", None), check_vma=False
    )
```

time: 163 us -> 21.5 us (0.13)
  the two profiles are of different devices: /device:TPU:103 before, /device:TPU:393 now
where the time goes in v4:
time: 21.5 us; the launch traced here: 21.4 us
  Pallas kernels  20.7 us (96%)
  local copies, waits for them, and re-layouts  0.72 us (3%)
    pallas_call x1, Pallas kernels, local(): pl.pallas_call(kernel, out_shape=pltpu.VMEM(diffusivity.shape, f32), in_s...  20.7 us
    unnamed x1, local copies, waits for them, and re-layouts  0.72 us

profile of v4, /device:TPU:393, one launch (start us, length us, event | category | flops | bytes accessed | tf_op | source)
XLA Modules:
  0.0 21.4 jit_solution(17911323734279580754)
XLA Ops:
  0.0 20.7 %regrid_smooth.1 = f32[9,4,16,128]{3,2,1,0:T(8,128)S(1)} custom-call(s32[1,2,64]{2,1,0:T(2,128)} %own_hbm.1, f32[2,9,4,16,128]{4,3,2,1,0:T(8,128)} %old_ref.1, bf16[9,4,16,128]{3,2,1,0:T(8,128)(2,1)} %dif_ref.1), custom_call_target="tpu_custom_call" | custom-call | tf_op jit(solution)/shard_map/regrid_smooth/pallas_call | solution.py:426
  20.7 0.7 %copy.5 = f32[9,4,16,128]{3,2,1,0:T(8,128)} copy(f32[9,4,16,128]{3,2,1,0:T(8,128)S(1)} %regrid_smooth.1) | data formatting | bytes 589824

commit v5 on v4

--- a/solution.py
+++ b/solution.py
@@ -71,7 +71,7 @@
 
 
 def kernel(own_hbm, old_ref, dif_ref, res, own_ref, old, far, via, near, mine, merged, got, kept_own, box, beside,
-           edge, got_edge, tips, tip, corner, corner_f32, scl_cand, scl_recv, scl_own, scl_got,
+           edge, got_edge, tips, tip, corner, corner_f32, scl_f32, scl_cand, scl_recv, scl_set, scl_beside, scl,
            dif, dif_edge, dif_beside, dif_got, dif_corner, coef, slab, cur, wts, pool,
            sem_in, sem_out, sem_far, sem_regrid, sem_halo, sem_scl, sem_dif):
     species = dif_ref.shape[0]
@@ -144,7 +144,7 @@
                 def _():
                     wait_units(sem, units(ns, ne))
 
-    scl_units = scl_own.shape[0] // 8
+    scl_units = scl_set.shape[1] // 16
 
     def halo_units(ns, ne):
         return ne * size + ns * ne * pairs + ns * 4 * size
@@ -175,9 +175,10 @@
         return out + [to_side(box.at[part(k)], beside.at[i, part(k)], sem_halo.at[k], i) for i in range(2)]
 
     scl_messages = [message(scl_cand.at[d - 1], scl_recv.at[BLOCK - d], sem_scl.at[0], ring[d]) for d in range(1, BLOCK)]
-    scl_around = [to_side(scl_own, scl_got.at[i, 0], sem_scl.at[1], i) for i in range(2)]
-    scl_around += [to_end(scl_own, scl_got.at[2, 1 + j], sem_scl.at[1], j) for j in range(2)]
-    scl_around += [to_diagonal(scl_own, scl_got.at[i, 1 + j], sem_scl.at[1], i, j) for i in range(2) for j in range(2)]
+    scl_around = [to_side(scl_set.at[0], scl_beside.at[i, 0], sem_scl.at[1], i) for i in range(2)]
+    scl_around += [to_end(scl_set.at[0], scl_set.at[1 + j], sem_scl.at[1], j) for j in range(2)]
+    scl_around += [to_diagonal(scl_set.at[0], scl_beside.at[i, 1 + j], sem_scl.at[1], i, j)
+                   for i in range(2) for j in range(2)]
     dif_ends = [to_end(dif_edge.at[e], dif_got.at[e], sem_dif.at[0], e) for e in range(2)]
     dif_sides = [to_side(dif, dif_beside.at[i], sem_dif.at[1], i) for i in range(2)]
     dif_corners = [to_side(dif_got, dif_corner.at[i], sem_dif.at[1], i) for i in range(2)]
@@ -204,7 +205,7 @@
             m = jnp.maximum(jnp.maximum(jnp.abs(layers[0]), jnp.abs(layers[1])),
                             jnp.maximum(jnp.abs(layers[2]), jnp.abs(layers[3])))
             m = jnp.maximum(jnp.max(m, axis=0, keepdims=True), 1e-30)
-            scale = m * (1.0 / LEVELS)
+            scale = (m * (1.004 / LEVELS)).astype(jnp.bfloat16).astype(jnp.float32)
             inv = 1.0 / scale
             rows = [jnp.round(v * inv).astype(jnp.int32) for v in layers]
             codes.append([jnp.concatenate(rows[2 * h:2 * h + 2], 0) for h in range(2)])
@@ -219,20 +220,19 @@
             mine[h, s] = code((3, 1)[h], h)
             kept_own[h, s] = code(0, h)
         for d in range(BLOCK):
-            scale = jnp.where(first_slot[d], scales[0], scales[1])
-            if d:
-                scl_cand[d - 1, pl.ds(s, 1)] = scale
-            else:
-                scl_recv[0, pl.ds(s, 1)] = scale
+            scl_f32[d, pl.ds(s, 1)] = jnp.where(first_slot[d], scales[0], scales[1])
 
     each(species, encode)
+    for d in range(1, BLOCK):
+        scl_cand[d - 1] = scl_f32[d].astype(jnp.bfloat16)
+    scl_recv[0] = scl_f32[0].astype(jnp.bfloat16)
     dif_load.wait()
 
     pl.semaphore_wait(barrier, BLOCK - 1 + in_sides + in_ends + in_sides * in_ends)
 
     each(count, lambda k: start(far_messages(k)))
+    each(count, lambda k: start(near_messages(k)))
     start(scl_messages)
-    each(count, lambda k: start(near_messages(k)))
     start(dif_sides)
 
     def dif_pack(s):
@@ -254,8 +254,9 @@
     each(count, merge)
 
     wait_units(sem_scl.at[0], 3 * scl_units)
-    scl_own[...] = scl_recv[came]
+    scl_set[0] = scl_recv[came]
     start(scl_around)
+
     wait_around(sem_dif.at[0], lambda ns, ne: species * ne)
     start(dif_corners)
 
@@ -331,6 +332,11 @@
     each(species, weigh)
 
     wait_around(sem_scl.at[1], lambda ns, ne: scl_units * (ns + ne + ns * ne))
+    for block, i in ((0, 0), (1, None), (2, 1)):
+        rows = [(scl_set if i is None else scl_beside.at[i])[j].astype(jnp.float32) for j in range(3)]
+        scl[block, 0] = rows[0] if i is None else kept(has_side[i], rows[0])
+        for j in range(2):
+            scl[block, 1 + j] = kept(both(i, j), rows[1 + j])
 
     def smooth(k):
         wait_around(sem_halo.at[k], halo_units)
@@ -342,16 +348,13 @@
         for s in range(size):
             at = k * size + s
             for block, i in ((0, 0), (1, None), (2, 1)):
+                scales = [scl[block, j, pl.ds(at, 1)] for j in range(3)]
+                q = (box[at] if i is None else beside[i, at]).astype(jnp.int32).astype(jnp.float32) * scales[0]
                 if i is None:
-                    q = box[at].astype(jnp.int32).astype(jnp.float32) * scl_own[pl.ds(at, 1)]
-                    halo = dict(enumerate(unpack_edges(*[
-                        got_edge[j, at].astype(jnp.int32).astype(jnp.float32)
-                        * kept(has_end[j], scl_got[2, 1 + j, pl.ds(at, 1)]) for j in range(2)])))
+                    tiles = [got_edge[j, at].astype(jnp.int32).astype(jnp.float32) * scales[1 + j] for j in range(2)]
+                    halo = dict(enumerate(unpack_edges(*tiles)))
                 else:
-                    q = beside[i, at].astype(jnp.int32).astype(jnp.float32)
-                    q = q * kept(has_side[i], scl_got[i, 0, pl.ds(at, 1)])
-                    halo = unpack_tips(i, *[corner_f32[i, j, s] * kept(both(i, j), scl_got[i, 1 + j, pl.ds(at, 1)])
-                                            for j in range(2)])
+                    halo = unpack_tips(i, *[corner_f32[i, j, s] * scales[1 + j] for j in range(2)])
                 for a in range(4):
                     slab[s, 4 * block + a, 0:16] = q[16 * a:16 * a + 16]
                     if a in halo:
@@ -385,7 +388,7 @@
     species = diffusivity.shape[0]
     size = 3 if species % 3 == 0 else 1
     count = species // size
-    pairs, padded = (size + 1) // 2, (species + 7) // 8 * 8
+    pairs, padded = (size + 1) // 2, (species + 15) // 16 * 16
     units = 18 * species + 3 * padded // 8 + padded + 14 * species + count * (10 * size + 4 * pairs)
     i16, i32, bf16, f32 = jnp.int16, jnp.int32, jnp.bfloat16, jnp.float32
     dma = pltpu.SemaphoreType.DMA
@@ -404,9 +407,11 @@
         pltpu.VMEM((count, 2, 2, pairs, 16, 128), i16),
         pltpu.VMEM((count, 2, 2, pairs, 16, 128), i16),
         pltpu.VMEM((2, 2, 2 * pairs, 8, 128), f32),
-        pltpu.VMEM((3, padded, 128), f32),
         pltpu.VMEM((4, padded, 128), f32),
-        pltpu.VMEM((padded, 128), f32),
+        pltpu.VMEM((3, padded, 128), bf16),
+        pltpu.VMEM((4, padded, 128), bf16),
+        pltpu.VMEM((3, padded, 128), bf16),
+        pltpu.VMEM((2, 3, padded, 128), bf16),
         pltpu.VMEM((3, 3, padded, 128), f32),
         pltpu.VMEM((species, 4, 16, 128), bf16),
         pltpu.VMEM((2, species, 16, 128), bf16),

time: 21.5 us -> 21 us (0.977)
  Pallas kernels: 20.7 us -> 20.1 us
    pallas_call x1, Pallas kernels: 20.7 us -> 20.1 us  [local(): pl.pallas_call(kernel, out_shape=pltpu.VMEM(diffusivity.shape, f32), in_s...]
where the time goes in v5:
time: 21 us; the launch traced here: 20.8 us
  Pallas kernels  20.1 us (96%)
  local copies, waits for them, and re-layouts  0.72 us (3%)
    pallas_call x1, Pallas kernels, local(): pl.pallas_call(kernel, out_shape=pltpu.VMEM(diffusivity.shape, f32), in_s...  20.1 us
    unnamed x1, local copies, waits for them, and re-layouts  0.72 us

profile of v5, /device:TPU:393, one launch (start us, length us, event | category | flops | bytes accessed | tf_op | source)
XLA Modules:
  0.0 20.8 jit_solution(18345945437938512193)
XLA Ops:
  0.0 20.1 %regrid_smooth.1 = f32[9,4,16,128]{3,2,1,0:T(8,128)S(1)} custom-call(s32[1,2,64]{2,1,0:T(2,128)} %own_hbm.1, f32[2,9,4,16,128]{4,3,2,1,0:T(8,128)} %old_ref.1, bf16[9,4,16,128]{3,2,1,0:T(8,128)(2,1)} %dif_ref.1), custom_call_target="tpu_custom_call" | custom-call | tf_op jit(solution)/shard_map/regrid_smooth/pallas_call | solution.py:431
  20.1 0.7 %copy.5 = f32[9,4,16,128]{3,2,1,0:T(8,128)} copy(f32[9,4,16,128]{3,2,1,0:T(8,128)S(1)} %regrid_smooth.1) | data formatting | bytes 589824

commit v6 on v5

--- a/solution.py
+++ b/solution.py
@@ -297,39 +297,43 @@
 
     wait_around(sem_dif.at[1], lambda ns, ne: 6 * species * ns)
 
-    def weigh(at):
-        for block, i in ((0, 0), (1, None), (2, 1)):
-            for a in range(4):
-                if i is None:
-                    coef[4 * block + a, 0:16] = dif[at, a].astype(jnp.float32)
-                else:
-                    coef[4 * block + a, 0:16] = kept(has_side[i], dif_beside[i, at, a].astype(jnp.float32))
-            tiles = [dif_got[j, at] if i is None else dif_corner[i, j, at] for j in range(2)]
-            halo = unpack_edges(*[kept(both(i, j), tiles[j].astype(jnp.float32)) for j in range(2)])
-            for a in range(4):
-                coef[4 * block + a, 16:24] = halo[a]
-        c = coef[0]
-        from_layer = None
-        for a in range(11):
-            above = coef[a + 1]
-            to_layer = 0.25 * (c + above)
-            wts[at, a, 0] = to_layer
-            if a:
-                to_row = 0.25 * (c + pltpu.roll(c, ZROWS - 1, 0))
-                to_column = 0.25 * (c + pltpu.roll(c, 127, 1))
-                total = (to_layer + from_layer) + (to_row + pltpu.roll(to_row, 1, 0))
-                total = total + (to_column + pltpu.roll(to_column, 1, 1))
-                inverse = in_rows / (1.0 + total)
-                if a < 4:
-                    inverse = inverse * in_side[0]
-                elif a > 7:
-                    inverse = inverse * in_side[1]
-                wts[at, a, 1] = to_row
-                wts[at, a, 2] = to_column
-                wts[at, a, 3] = inverse
-            from_layer, c = to_layer, above
-
-    each(species, weigh)
+    def weigh(k):
+        for s in range(size):
+            at = k * size + s
+            for block, i in ((0, 0), (1, None), (2, 1)):
+                for a in range(4):
+                    if i is None:
+                        coef[s, 4 * block + a, 0:16] = dif[at, a].astype(jnp.float32)
+                    else:
+                        coef[s, 4 * block + a, 0:16] = kept(has_side[i], dif_beside[i, at, a].astype(jnp.float32))
+                tiles = [dif_got[j, at] if i is None else dif_corner[i, j, at] for j in range(2)]
+                halo = unpack_edges(*[kept(both(i, j), tiles[j].astype(jnp.float32)) for j in range(2)])
+                for a in range(4):
+                    coef[s, 4 * block + a, 16:24] = halo[a]
+        for s in range(size):
+            at = k * size + s
+            c = coef[s, 0]
+            from_layer = None
+            for a in range(11):
+                above = coef[s, a + 1]
+                to_layer = 0.25 * (c + above)
+                wts[at, a, 0] = to_layer
+                if a:
+                    to_row = 0.25 * (c + pltpu.roll(c, ZROWS - 1, 0))
+                    to_column = 0.25 * (c + pltpu.roll(c, 127, 1))
+                    total = (to_layer + from_layer) + (to_row + pltpu.roll(to_row, 1, 0))
+                    total = total + (to_column + pltpu.roll(to_column, 1, 1))
+                    inverse = in_rows / (1.0 + total)
+                    if a < 4:
+                        inverse = inverse * in_side[0]
+                    elif a > 7:
+                        inverse = inverse * in_side[1]
+                    wts[at, a, 1] = to_row
+                    wts[at, a, 2] = to_column
+                    wts[at, a, 3] = inverse
+                from_layer, c = to_layer, above
+
+    each(count, weigh)
 
     wait_around(sem_scl.at[1], lambda ns, ne: scl_units * (ns + ne + ns * ne))
     for block, i in ((0, 0), (1, None), (2, 1)):
@@ -418,7 +422,7 @@
         pltpu.VMEM((2, species, 4, 16, 128), bf16),
         pltpu.VMEM((2, species, 16, 128), bf16),
         pltpu.VMEM((2, 2, species, 16, 128), bf16),
-        pltpu.VMEM((12, ZROWS, 128), f32),
+        pltpu.VMEM((size, 12, ZROWS, 128), f32),
         pltpu.VMEM((size, 12, ZROWS, 128), f32),
         pltpu.VMEM((2, size, 12, ZROWS, 128), f32),
         pltpu.VMEM((species, 11, 4, ZROWS, 128), f32),

time: 21 us -> 21 us (level)
  no operation moved by 1% of the time
where the time goes in v6:
time: 21 us; the launch traced here: 20.8 us
  Pallas kernels  20.1 us (96%)
  local copies, waits for them, and re-layouts  0.72 us (3%)
    pallas_call x1, Pallas kernels, local(): pl.pallas_call(kernel, out_shape=pltpu.VMEM(diffusivity.shape, f32), in_s...  20.1 us
    unnamed x1, local copies, waits for them, and re-layouts  0.72 us

profile of v6, /device:TPU:393, one launch (start us, length us, event | category | flops | bytes accessed | tf_op | source)
XLA Modules:
  0.0 20.8 jit_solution(5104611119311535046)
XLA Ops:
  0.0 20.1 %regrid_smooth.1 = f32[9,4,16,128]{3,2,1,0:T(8,128)S(1)} custom-call(s32[1,2,64]{2,1,0:T(2,128)} %own_hbm.1, f32[2,9,4,16,128]{4,3,2,1,0:T(8,128)} %old_ref.1, bf16[9,4,16,128]{3,2,1,0:T(8,128)(2,1)} %dif_ref.1), custom_call_target="tpu_custom_call" | custom-call | tf_op jit(solution)/shard_map/regrid_smooth/pallas_call | solution.py:435
  20.1 0.7 %copy.5 = f32[9,4,16,128]{3,2,1,0:T(8,128)} copy(f32[9,4,16,128]{3,2,1,0:T(8,128)S(1)} %regrid_smooth.1) | data formatting | bytes 589824

commit v7 on v6

--- a/solution.py
+++ b/solution.py
@@ -231,8 +231,6 @@
     pl.semaphore_wait(barrier, BLOCK - 1 + in_sides + in_ends + in_sides * in_ends)
 
     each(count, lambda k: start(far_messages(k)))
-    each(count, lambda k: start(near_messages(k)))
-    start(scl_messages)
     start(dif_sides)
 
     def dif_pack(s):
@@ -242,6 +240,8 @@
 
     each(species, dif_pack)
     start(dif_ends)
+    each(count, lambda k: start(near_messages(k)))
+    start(scl_messages)
 
     def merge(k):
         wait_units(sem_far.at[k], 4 * size)

time: 21 us -> 21 us (level)
  no operation moved by 1% of the time
where the time goes in v7:
time: 21 us; the launch traced here: 20.8 us
  Pallas kernels  20.1 us (96%)
  local copies, waits for them, and re-layouts  0.72 us (3%)
    pallas_call x1, Pallas kernels, local(): pl.pallas_call(kernel, out_shape=pltpu.VMEM(diffusivity.shape, f32), in_s...  20.1 us
    unnamed x1, local copies, waits for them, and re-layouts  0.72 us

profile of v7, /device:TPU:393, one launch (start us, length us, event | category | flops | bytes accessed | tf_op | source)
XLA Modules:
  0.0 20.8 jit_solution(1346449006813143249)
XLA Ops:
  0.0 20.1 %regrid_smooth.1 = f32[9,4,16,128]{3,2,1,0:T(8,128)S(1)} custom-call(s32[1,2,64]{2,1,0:T(2,128)} %own_hbm.1, f32[2,9,4,16,128]{4,3,2,1,0:T(8,128)} %old_ref.1, bf16[9,4,16,128]{3,2,1,0:T(8,128)(2,1)} %dif_ref.1), custom_call_target="tpu_custom_call" | custom-call | tf_op jit(solution)/shard_map/regrid_smooth/pallas_call | solution.py:435
  20.1 0.7 %copy.5 = f32[9,4,16,128]{3,2,1,0:T(8,128)} copy(f32[9,4,16,128]{3,2,1,0:T(8,128)S(1)} %regrid_smooth.1) | data formatting | bytes 589824

commit v8 on v6

--- a/solution.py
+++ b/solution.py
@@ -169,10 +169,10 @@
         return [message(merged.at[h, part(k)], got.at[0, h, part(k)], sem_regrid.at[k], ahead[h]) for h in range(2)]
 
     def halo_messages(k):
-        out = [to_end(edge.at[e, part(k)], got_edge.at[e, part(k)], sem_halo.at[k], e) for e in range(2)]
-        out += [to_diagonal(tip.at[k, i, e], corner.at[k, i, e], sem_halo.at[k], i, e)
-                for i in range(2) for e in range(2)]
-        return out + [to_side(box.at[part(k)], beside.at[i, part(k)], sem_halo.at[k], i) for i in range(2)]
+        out = [to_side(box.at[part(k)], beside.at[i, part(k)], sem_halo.at[k], i) for i in range(2)]
+        out += [to_end(edge.at[e, part(k)], got_edge.at[e, part(k)], sem_halo.at[k], e) for e in range(2)]
+        return out + [to_diagonal(tip.at[k, i, e], corner.at[k, i, e], sem_halo.at[k], i, e)
+                      for i in range(2) for e in range(2)]
 
     scl_messages = [message(scl_cand.at[d - 1], scl_recv.at[BLOCK - d], sem_scl.at[0], ring[d]) for d in range(1, BLOCK)]
     scl_around = [to_side(scl_set.at[0], scl_beside.at[i, 0], sem_scl.at[1], i) for i in range(2)]

time: 21 us -> 21 us (level)
  no operation moved by 1% of the time
where the time goes in v8:
time: 21 us; the launch traced here: 20.9 us
  Pallas kernels  20.1 us (96%)
  local copies, waits for them, and re-layouts  0.72 us (3%)
    pallas_call x1, Pallas kernels, local(): pl.pallas_call(kernel, out_shape=pltpu.VMEM(diffusivity.shape, f32), in_s...  20.1 us
    unnamed x1, local copies, waits for them, and re-layouts  0.72 us

profile of v8, /device:TPU:393, one launch (start us, length us, event | category | flops | bytes accessed | tf_op | source)
XLA Modules:
  0.0 20.9 jit_solution(14626719695952994078)
XLA Ops:
  0.0 20.1 %regrid_smooth.1 = f32[9,4,16,128]{3,2,1,0:T(8,128)S(1)} custom-call(s32[1,2,64]{2,1,0:T(2,128)} %own_hbm.1, f32[2,9,4,16,128]{4,3,2,1,0:T(8,128)} %old_ref.1, bf16[9,4,16,128]{3,2,1,0:T(8,128)(2,1)} %dif_ref.1), custom_call_target="tpu_custom_call" | custom-call | tf_op jit(solution)/shard_map/regrid_smooth/pallas_call | solution.py:435
  20.1 0.7 %copy.5 = f32[9,4,16,128]{3,2,1,0:T(8,128)} copy(f32[9,4,16,128]{3,2,1,0:T(8,128)S(1)} %regrid_smooth.1) | data formatting | bytes 589824
